TPU v7x, 128 devices: a whole 4x4x4 slice. The times are simulated.
128 devices in a mesh: ctx: 16 (over y, z_hi, core), exp: 8 (over z_lo, x).
Axes of the slice: x: 4, y: 4, z: 4 (z_hi: 2, z_lo: 2; z = z_hi * 2 + z_lo), core: 2. Of those that a mesh axis runs over, the one named last changes fastest.
Arguments:
- queries: bfloat16 [2048, 6144], P('ctx', 'exp'), may hold values from -16 to 16
- keys: bfloat16 [2048, 1024], P('ctx', 'exp'), may hold values from -4 to 4
- values: bfloat16 [2048, 1024], P('ctx', 'exp'), may hold values from -6 to 6
- residual: bfloat16 [2048, 6144], P('ctx', 'exp'), may hold values from -16 to 16
- ln_gain: float32 [6144], P('exp'), may hold values from 0.5 to 1.5
- out_weight: bfloat16 [6144, 6144], P('exp'), may hold values from -0.3125 to 0.3125
- gate_weight: bfloat16 [8, 6144, 5376], P('exp', None, 'ctx'), may hold values from -0.078125 to 0.078125
- up_weight: bfloat16 [8, 6144, 5376], P('exp', None, 'ctx'), may hold values from -0.078125 to 0.078125
- down_weight: bfloat16 [8, 5376, 6144], P('exp', 'ctx'), may hold values from -0.078125 to 0.078125
- expert_ids: int32 [2048, 4], P('ctx'), may hold values from 0 to 7, all different within a row; in each aligned block of 128 rows (0 to 127, 128 to 255, ...) at most 80 rows name the same one
- gate_scores: float32 [2048, 4], P('ctx'), may hold values from 0.1 to 1
Outputs:
- mixed: bfloat16 [2048, 6144], P('ctx', 'exp')
Inputs may be any that keep to these rules, and one draw needn't show every extreme that they name: `expert_ids`: each token names 4 different experts. Among the 128 tokens of one context shard (aligned blocks of rows) no expert is named more than 80 times, and in every draw some expert is named exactly 80 times in some shard.
All inputs are finite; a program needn't handle non-finite values.
Results may differ from a plain program's by a relative error of at most 0.0095.
Values may be sent and summed in bfloat16 or wider, within the bound.
No kernel may reach another device: no remote copies, remote signals or barrier semaphores. Data moves between devices by JAX's collectives and lax.ppermute only.
A program may use at most 128 MiB of HBM per device.

v0:
```python
import jax
import jax.numpy as jnp
from jax import lax
from jax.sharding import PartitionSpec as P

D = 6144
HD = 128
EXPERTS = 8
TOPK = 4
CAP = 80


EPS = 1e-05


def shifted(block, axis, distance):
    devices = range(lax.axis_size(axis))
    route = [(i - distance, i) for i in devices if i - distance in devices]
    return lax.ppermute(block, axis, route)


def attend_block(carry, q_view, q_pos, key_block, value_block, key_start):
    top, total, summed = carry
    count = key_block.shape[0]
    kv_local = q_view.shape[1]
    key_view = key_block.reshape(count, kv_local, HD)
    value_view = value_block.reshape(count, kv_local, HD)
    scores = jnp.einsum(
        "tkgd,skd->kgts", q_view, key_view, preferred_element_type=jnp.float32
    ) * HD ** (-0.5)
    key_pos = key_start + lax.iota(jnp.int32, count)
    keep = (key_pos[None, :] <= q_pos[:, None]) & (key_start >= 0)
    scores = jnp.where(keep, scores, -1e30)
    new_top = jnp.maximum(top, jnp.max(scores, axis=3))
    factor = jnp.exp(top - new_top)
    expw = jnp.where(keep, jnp.exp(scores - new_top[..., None]), 0.0)
    total = total * factor + jnp.sum(expw, axis=3)
    summed = summed * factor[..., None] + jnp.einsum(
        "kgts,skd->kgtd", expw.astype(jnp.bfloat16), value_view, preferred_element_type=jnp.float32
    )
    return (new_top, total, summed)


def body(
    queries,
    keys,
    values,
    residual,
    ln_gain,
    out_weight,
    gate_weight,
    up_weight,
    down_weight,
    expert_ids,
    gate_scores,
):
    tok = queries.shape[0]
    kv_local = keys.shape[1] // HD
    q_local = queries.shape[1] // HD
    group = q_local // kv_local
    ctx_index = lax.axis_index("ctx")
    q_pos = ctx_index * tok + lax.iota(jnp.int32, tok)
    q_view = queries.reshape(tok, kv_local, group, HD)
    start_state = (
        jnp.full((kv_local, group, tok), -1e30, jnp.float32),
        jnp.zeros((kv_local, group, tok), jnp.float32),
        jnp.zeros((kv_local, group, tok, HD), jnp.float32),
    )
    state = attend_block(start_state, q_view, q_pos, keys, values, ctx_index * tok)

    def cycle_step(step, loop_state):
        blocks, carry = loop_state
        blocks = shifted(blocks, "ctx", 1)
        carry = attend_block(carry, q_view, q_pos, blocks[0], blocks[1], (ctx_index - step) * tok)
        return (blocks, carry)

    paired = jnp.stack((keys, values))
    paired, state = lax.fori_loop(1, lax.axis_size("ctx"), cycle_step, (paired, state))
    attended = (
        (state[2] / state[1][..., None])
        .transpose(2, 0, 1, 3)
        .reshape(tok, q_local * HD)
        .astype(jnp.bfloat16)
    )
    term = jnp.dot(attended, out_weight, preferred_element_type=jnp.float32)
    width = residual.shape[1]
    projected = lax.psum_scatter(term, "exp", scatter_dimension=1, tiled=True)
    hidden = residual.astype(jnp.float32) + projected
    sums = lax.psum((jnp.sum(hidden, axis=1), jnp.sum(hidden * hidden, axis=1)), "exp")
    mean = sums[0] / D
    second = sums[1] / D
    scale_rows = lax.rsqrt(second - mean * mean + EPS)
    normed = ((hidden - mean[:, None]) * scale_rows[:, None] * ln_gain[None, :]).astype(
        jnp.bfloat16
    )
    expert_range = lax.iota(jnp.int32, EXPERTS)
    member = jnp.sum(
        (expert_ids[:, :, None] == expert_range[None, None, :]).astype(jnp.float32), axis=1
    )
    lower = (
        lax.broadcasted_iota(jnp.int32, (tok, tok), 1)
        < lax.broadcasted_iota(jnp.int32, (tok, tok), 0)
    ).astype(jnp.float32)
    slot_of = jnp.dot(lower, member, preferred_element_type=jnp.float32).astype(jnp.int32)
    slot_range = lax.iota(jnp.int32, CAP)
    placing = (member.T[:, None, :] > 0.5) & (slot_of.T[:, None, :] == slot_range[None, :, None])
    outgoing = jnp.einsum(
        "est,tf->esf", placing.astype(jnp.bfloat16), normed, preferred_element_type=jnp.float32
    ).astype(jnp.bfloat16)
    local_experts = gate_weight.shape[0]
    arrived = lax.all_to_all(outgoing, "exp", split_axis=0, concat_axis=2, tiled=True)
    routed = lax.all_gather(arrived.reshape(local_experts * CAP, D), "ctx", axis=0, tiled=True)
    block = routed.reshape(-1, local_experts, CAP, D)
    gate_part = jnp.einsum("necd,edf->necf", block, gate_weight, preferred_element_type=jnp.float32)
    up_part = jnp.einsum("necd,edf->necf", block, up_weight, preferred_element_type=jnp.float32)
    act = (jax.nn.silu(gate_part) * up_part).astype(jnp.bfloat16)
    result = jnp.einsum("necf,efd->necd", act, down_weight, preferred_element_type=jnp.float32)
    expert_sums = lax.psum_scatter(
        result.reshape(lax.axis_size("ctx") * (local_experts * CAP), D).astype(jnp.bfloat16),
        "ctx",
        scatter_dimension=0,
        tiled=True,
    )
    back = expert_sums.reshape(local_experts, CAP, D)
    outputs = lax.all_to_all(back, "exp", split_axis=2, concat_axis=0, tiled=True)
    flat = outputs.reshape(EXPERTS * CAP, width)
    slot_taken = jnp.take_along_axis(slot_of, expert_ids, axis=1)
    position = (expert_ids * CAP + slot_taken).reshape(-1)
    picked = jnp.take(flat, position, axis=0).reshape(tok, TOPK, width).astype(jnp.float32)
    share = gate_scores / jnp.sum(gate_scores, axis=1, keepdims=True)
    moe = jnp.sum(share[:, :, None] * picked, axis=1)
    return (hidden + moe).astype(jnp.bfloat16)


def solution(mesh):
    return jax.shard_map(
        body,
        mesh=mesh,
        in_specs=(
            P("ctx", "exp"),
            P("ctx", "exp"),
            P("ctx", "exp"),
            P("ctx", "exp"),
            P("exp"),
            P("exp", None),
            P("exp", None, "ctx"),
            P("exp", None, "ctx"),
            P("exp", "ctx", None),
            P("ctx", None),
            P("ctx", None),
        ),
        out_specs=P("ctx", "exp"),
        check_vma=False,
    )
```

profile of v0, /device:TPU:0, one launch (start us, length us, event | category | flops | bytes accessed | tf_op | source)
XLA Modules:
  0.0 597.3 jit_solution(12071506616374748388)
XLA Ops:
  10.8 116.1 %while.20 = (s32[]{:T(128)}, bf16[2,128,128]{2,1,0:T(8,128)(2,1)S(1)}, f32[1,6,128]{2,1,0:T(8,128)S(1)}, f32[1,6,128]{2,1,0:T(8,128)S(1)}, f32[1,6,128,128]{3,2,...) while((s32[]{:T(128)}, ...), condition=%wide.region_5.6_spmd.clone, body=%wide.region_2.5_spmd.clone.sunk | while | flops 51448324 | bytes 2740415 | solution.py:78
  13.7 7.0 %collective-permute-start = (bf16[2,128,128]{2,1,0:T(8,128)(2,1)S(1)}, bf16[2,128,128]{2,1,0:T(8,128)(2,1)S(1)}, u32[]{:S(2)}, u32[]{:S(2)}) collective-permute-start(bf16[2,128,128]{2,1,0:T(8,128)(2,1)S(1)} %get-tuple-element.314), channel_id=1, source_target_pairs={{0,8},{8,16},{16,24},{24,32},{32,40},{40,48},{48,56},{56,64},{64,7... | collective-permute-start | bytes 196616 | tf_op jit(solution)/shard_map/while/body/eval_jaxpr/ppermute | solution.py:19
  22.4 6.2 %collective-permute-start = (bf16[2,128,128]{2,1,0:T(8,128)(2,1)S(1)}, bf16[2,128,128]{2,1,0:T(8,128)(2,1)S(1)}, u32[]{:S(2)}, u32[]{:S(2)}) collective-permute-start(bf16[2,128,128]{2,1,0:T(8,128)(2,1)S(1)} %get-tuple-element.314), channel_id=1, source_target_pairs={{0,8},{8,16},{16,24},{24,32},{32,40},{40,48},{48,56},{56,64},{64,7... | collective-permute-start | bytes 196616 | tf_op jit(solution)/shard_map/while/body/eval_jaxpr/ppermute | solution.py:19
  30.3 6.2 %collective-permute-start = (bf16[2,128,128]{2,1,0:T(8,128)(2,1)S(1)}, bf16[2,128,128]{2,1,0:T(8,128)(2,1)S(1)}, u32[]{:S(2)}, u32[]{:S(2)}) collective-permute-start(bf16[2,128,128]{2,1,0:T(8,128)(2,1)S(1)} %get-tuple-element.314), channel_id=1, source_target_pairs={{0,8},{8,16},{16,24},{24,32},{32,40},{40,48},{48,56},{56,64},{64,7... | collective-permute-start | bytes 196616 | tf_op jit(solution)/shard_map/while/body/eval_jaxpr/ppermute | solution.py:19
  38.1 6.2 %collective-permute-start = (bf16[2,128,128]{2,1,0:T(8,128)(2,1)S(1)}, bf16[2,128,128]{2,1,0:T(8,128)(2,1)S(1)}, u32[]{:S(2)}, u32[]{:S(2)}) collective-permute-start(bf16[2,128,128]{2,1,0:T(8,128)(2,1)S(1)} %get-tuple-element.314), channel_id=1, source_target_pairs={{0,8},{8,16},{16,24},{24,32},{32,40},{40,48},{48,56},{56,64},{64,7... | collective-permute-start | bytes 196616 | tf_op jit(solution)/shard_map/while/body/eval_jaxpr/ppermute | solution.py:19
  46.0 6.2 %collective-permute-start = (bf16[2,128,128]{2,1,0:T(8,128)(2,1)S(1)}, bf16[2,128,128]{2,1,0:T(8,128)(2,1)S(1)}, u32[]{:S(2)}, u32[]{:S(2)}) collective-permute-start(bf16[2,128,128]{2,1,0:T(8,128)(2,1)S(1)} %get-tuple-element.314), channel_id=1, source_target_pairs={{0,8},{8,16},{16,24},{24,32},{32,40},{40,48},{48,56},{56,64},{64,7... | collective-permute-start | bytes 196616 | tf_op jit(solution)/shard_map/while/body/eval_jaxpr/ppermute | solution.py:19
  53.8 6.2 %collective-permute-start = (bf16[2,128,128]{2,1,0:T(8,128)(2,1)S(1)}, bf16[2,128,128]{2,1,0:T(8,128)(2,1)S(1)}, u32[]{:S(2)}, u32[]{:S(2)}) collective-permute-start(bf16[2,128,128]{2,1,0:T(8,128)(2,1)S(1)} %get-tuple-element.314), channel_id=1, source_target_pairs={{0,8},{8,16},{16,24},{24,32},{32,40},{40,48},{48,56},{56,64},{64,7... | collective-permute-start | bytes 196616 | tf_op jit(solution)/shard_map/while/body/eval_jaxpr/ppermute | solution.py:19
  61.7 6.2 %collective-permute-start = (bf16[2,128,128]{2,1,0:T(8,128)(2,1)S(1)}, bf16[2,128,128]{2,1,0:T(8,128)(2,1)S(1)}, u32[]{:S(2)}, u32[]{:S(2)}) collective-permute-start(bf16[2,128,128]{2,1,0:T(8,128)(2,1)S(1)} %get-tuple-element.314), channel_id=1, source_target_pairs={{0,8},{8,16},{16,24},{24,32},{32,40},{40,48},{48,56},{56,64},{64,7... | collective-permute-start | bytes 196616 | tf_op jit(solution)/shard_map/while/body/eval_jaxpr/ppermute | solution.py:19
  69.5 6.2 %collective-permute-start = (bf16[2,128,128]{2,1,0:T(8,128)(2,1)S(1)}, bf16[2,128,128]{2,1,0:T(8,128)(2,1)S(1)}, u32[]{:S(2)}, u32[]{:S(2)}) collective-permute-start(bf16[2,128,128]{2,1,0:T(8,128)(2,1)S(1)} %get-tuple-element.314), channel_id=1, source_target_pairs={{0,8},{8,16},{16,24},{24,32},{32,40},{40,48},{48,56},{56,64},{64,7... | collective-permute-start | bytes 196616 | tf_op jit(solution)/shard_map/while/body/eval_jaxpr/ppermute | solution.py:19
  77.3 6.2 %collective-permute-start = (bf16[2,128,128]{2,1,0:T(8,128)(2,1)S(1)}, bf16[2,128,128]{2,1,0:T(8,128)(2,1)S(1)}, u32[]{:S(2)}, u32[]{:S(2)}) collective-permute-start(bf16[2,128,128]{2,1,0:T(8,128)(2,1)S(1)} %get-tuple-element.314), channel_id=1, source_target_pairs={{0,8},{8,16},{16,24},{24,32},{32,40},{40,48},{48,56},{56,64},{64,7... | collective-permute-start | bytes 196616 | tf_op jit(solution)/shard_map/while/body/eval_jaxpr/ppermute | solution.py:19
  85.2 6.2 %collective-permute-start = (bf16[2,128,128]{2,1,0:T(8,128)(2,1)S(1)}, bf16[2,128,128]{2,1,0:T(8,128)(2,1)S(1)}, u32[]{:S(2)}, u32[]{:S(2)}) collective-permute-start(bf16[2,128,128]{2,1,0:T(8,128)(2,1)S(1)} %get-tuple-element.314), channel_id=1, source_target_pairs={{0,8},{8,16},{16,24},{24,32},{32,40},{40,48},{48,56},{56,64},{64,7... | collective-permute-start | bytes 196616 | tf_op jit(solution)/shard_map/while/body/eval_jaxpr/ppermute | solution.py:19
  93.0 6.2 %collective-permute-start = (bf16[2,128,128]{2,1,0:T(8,128)(2,1)S(1)}, bf16[2,128,128]{2,1,0:T(8,128)(2,1)S(1)}, u32[]{:S(2)}, u32[]{:S(2)}) collective-permute-start(bf16[2,128,128]{2,1,0:T(8,128)(2,1)S(1)} %get-tuple-element.314), channel_id=1, source_target_pairs={{0,8},{8,16},{16,24},{24,32},{32,40},{40,48},{48,56},{56,64},{64,7... | collective-permute-start | bytes 196616 | tf_op jit(solution)/shard_map/while/body/eval_jaxpr/ppermute | solution.py:19
  100.9 6.9 %collective-permute-start = (bf16[2,128,128]{2,1,0:T(8,128)(2,1)S(1)}, bf16[2,128,128]{2,1,0:T(8,128)(2,1)S(1)}, u32[]{:S(2)}, u32[]{:S(2)}) collective-permute-start(bf16[2,128,128]{2,1,0:T(8,128)(2,1)S(1)} %get-tuple-element.314), channel_id=1, source_target_pairs={{0,8},{8,16},{16,24},{24,32},{32,40},{40,48},{48,56},{56,64},{64,7... | collective-permute-start | bytes 196616 | tf_op jit(solution)/shard_map/while/body/eval_jaxpr/ppermute | solution.py:19
  109.5 7.1 %collective-permute-start = (bf16[2,128,128]{2,1,0:T(8,128)(2,1)S(1)}, bf16[2,128,128]{2,1,0:T(8,128)(2,1)S(1)}, u32[]{:S(2)}, u32[]{:S(2)}) collective-permute-start(bf16[2,128,128]{2,1,0:T(8,128)(2,1)S(1)} %get-tuple-element.314), channel_id=1, source_target_pairs={{0,8},{8,16},{16,24},{24,32},{32,40},{40,48},{48,56},{56,64},{64,7... | collective-permute-start | bytes 196616 | tf_op jit(solution)/shard_map/while/body/eval_jaxpr/ppermute | solution.py:19
  118.2 7.1 %collective-permute-start = (bf16[2,128,128]{2,1,0:T(8,128)(2,1)S(1)}, bf16[2,128,128]{2,1,0:T(8,128)(2,1)S(1)}, u32[]{:S(2)}, u32[]{:S(2)}) collective-permute-start(bf16[2,128,128]{2,1,0:T(8,128)(2,1)S(1)} %get-tuple-element.314), channel_id=1, source_target_pairs={{0,8},{8,16},{16,24},{24,32},{32,40},{40,48},{48,56},{56,64},{64,7... | collective-permute-start | bytes 196616 | tf_op jit(solution)/shard_map/while/body/eval_jaxpr/ppermute | solution.py:19
  127.2 6.8 %fusion.59 = f32[128,6144]{1,0:T(8,128)} fusion(bf16[128,768]{0,1:T(8,128)(2,1)S(1)} %bitcast.197, bf16[768,6144]{1,0:T(8,128)(2,1)} %param.18), kind=kOutput, calls=%fused_computation.98 | convolution fusion | flops 1207959552 | bytes 12779520 | tf_op jit(solution)/shard_map/dot_general | solution.py:85
  134.3 61.1 %reduce-scatter.3.cloned.1.call-done = f32[128,768]{1,0:T(8,128)} async-done(((f32[128,6144]{1,0:T(8,128)}), f32[128,768]{1,0:T(8,128)}) %reduce-scatter.3.cloned.1.call-update) | async-done | bytes 393232 | tf_op jit(solution)/shard_map/reduce_scatter | solution.py:87
  196.5 18.7 %all-reduce = (f32[128]{0:T(128)S(1)}, f32[128]{0:T(128)S(1)}) all-reduce(f32[128]{0:T(128)S(1)} %get-tuple-element.207, f32[128]{0:T(128)S(1)} %get-tuple-element.206), channel_id=1, replica_groups=mesh['ctx'=16,'exp'=8] {'exp'}, use_global_device_ids=true, to_apply=%region_12.13 | all-reduce | flops 256 | bytes 2048 | tf_op jit(solution)/shard_map/psum | solution.py:89
  216.8 13.6 %all_to_all.30 = bf16[8,80,768]{2,1,0:T(8,128)(2,1)S(1)} all-to-all(bf16[8,80,768]{2,1,0:T(8,128)(2,1)S(1)} %convolution_convert_fusion.1), channel_id=1, replica_groups=mesh['ctx'=16,'exp'=8] {'exp'}, dimensions={0} | all-to-all | bytes 1966080 | tf_op jit(solution)/shard_map/all_to_all | solution.py:111
  231.6 104.4 %all-gather.2.cloned.1.call-done = bf16[1280,6144]{1,0:T(8,128)(2,1)} async-done(((bf16[80,6144]{1,0:T(8,128)(2,1)}), bf16[1280,6144]{1,0:T(8,128)(2,1)}) %all-gather.2.cloned.1.call-update) | async-done | bytes 15728656 | tf_op jit(solution)/shard_map/all_gather | solution.py:112
  336.0 12.9 %fusion.18 = f32[16,80,336]{2,1,0:T(8,128)S(1)} fusion(bf16[16,80,6144]{2,1,0:T(8,128)(2,1)} %bitcast.203, bf16[1,6144,336]{1,2,0:T(8,128)(2,1)} %param.19), kind=kOutput, calls=%fused_computation.30 | convolution fusion | flops 5284823040 | bytes 21577728 | tf_op jit(solution)/shard_map/necd,edf->necf/dot_general | solution.py:114
  348.9 23.9 %convolution_convert_fusion = bf16[16,80,6144]{2,1,0:T(8,128)(2,1)} fusion(bf16[1,336,6144]{2,1,0:T(8,128)(2,1)} %param.21, bf16[16,80,6144]{2,1,0:T(8,128)(2,1)} %bitcast.204, bf16[1,6144,336]{1,2,0:T(8,128)(2,1)} %param.20, f32[16,80,336]{2,1,0:T(8,128)S(1)} %fusion.18), kind=kOutput, calls=%fused_computation.26 | convolution fusion | flops 10580090880 | bytes 41435136 | tf_op jit(solution)/shard_map/necf,efd->necd/dot_general | solution.py:117
  372.8 135.3 %reduce-scatter.5.cloned.1.call-done = bf16[80,6144]{1,0:T(8,128)(2,1)} async-done(((bf16[1280,6144]{1,0:T(8,128)(2,1)}), bf16[80,6144]{1,0:T(8,128)(2,1)}) %reduce-scatter.5.cloned.1.call-update) | async-done | bytes 983056 | tf_op jit(solution)/shard_map/reduce_scatter | solution.py:118
  508.1 6.7 %copy.107 = bf16[1,80,6144]{1,0,2:T(2,128)(2,1)S(1)} copy(bf16[1,80,6144]{2,1,0:T(8,128)(2,1)} %bitcast.198) | data formatting | bytes 1966080 | tf_op jit(solution)/shard_map/reshape | solution.py:124
  515.3 34.4 %reduce.8 = bf16[6144,80]{1,0:T(8,128)(2,1)} reduce(bf16[6144,1,80]{2,1,0:T(2,128)(2,1)S(1)} %bitcast.187, bf16[]{:T(256)} %broadcast.171), dimensions={1}, to_apply=%bitcast.152.reduce_sub_computation | reduce | bytes 1966082
  549.8 5.4 reshape.277
  555.1 4.3 all-to-all-start.1
  559.6 2.5 gather_fusion.1
  562.9 11.3 %all-to-all-done.1 = bf16[8,2,30720]{2,1,0:T(2,128)(2,1)} async-done(((bf16[8,2,30720]{2,1,0:T(2,128)(2,1)}), bf16[8,2,30720]{2,1,0:T(2,128)(2,1)}, u32[]{:S(2)}, u32[]{:S(2)}) %all-to-all-start.1) | async-done | bytes 983072 | tf_op jit(solution)/shard_map/all_to_all | solution.py:125
  574.2 5.6 reshape.278
  579.8 5.1 copy.108
  586.5 2.0 gather_fusion
  (207 shorter events, 38.6 us)
Async XLA Ops:
  6.5 188.9 %reduce-scatter.3.cloned.1.call-start = ((), (), s32[]{:S(2)}) async-start(), calls=%async_computation.4 | async-start | bytes 3538944 | tf_op jit(solution)/shard_map/reduce_scatter | solution.py:87
  10.8 2.2 collective-permute-start
  13.7 7.9 %collective-permute-start = (bf16[2,128,128]{2,1,0:T(8,128)(2,1)S(1)}, bf16[2,128,128]{2,1,0:T(8,128)(2,1)S(1)}, u32[]{:S(2)}, u32[]{:S(2)}) collective-permute-start(bf16[2,128,128]{2,1,0:T(8,128)(2,1)S(1)} %get-tuple-element.314), channel_id=1, source_target_pairs={{0,8},{8,16},{16,24},{24,32},{32,40},{40,48},{48,56},{56,64},{64,7... | collective-permute-start | bytes 196616 | tf_op jit(solution)/shard_map/while/body/eval_jaxpr/ppermute | solution.py:19
  22.4 7.1 %collective-permute-start = (bf16[2,128,128]{2,1,0:T(8,128)(2,1)S(1)}, bf16[2,128,128]{2,1,0:T(8,128)(2,1)S(1)}, u32[]{:S(2)}, u32[]{:S(2)}) collective-permute-start(bf16[2,128,128]{2,1,0:T(8,128)(2,1)S(1)} %get-tuple-element.314), channel_id=1, source_target_pairs={{0,8},{8,16},{16,24},{24,32},{32,40},{40,48},{48,56},{56,64},{64,7... | collective-permute-start | bytes 196616 | tf_op jit(solution)/shard_map/while/body/eval_jaxpr/ppermute | solution.py:19
  30.3 7.1 %collective-permute-start = (bf16[2,128,128]{2,1,0:T(8,128)(2,1)S(1)}, bf16[2,128,128]{2,1,0:T(8,128)(2,1)S(1)}, u32[]{:S(2)}, u32[]{:S(2)}) collective-permute-start(bf16[2,128,128]{2,1,0:T(8,128)(2,1)S(1)} %get-tuple-element.314), channel_id=1, source_target_pairs={{0,8},{8,16},{16,24},{24,32},{32,40},{40,48},{48,56},{56,64},{64,7... | collective-permute-start | bytes 196616 | tf_op jit(solution)/shard_map/while/body/eval_jaxpr/ppermute | solution.py:19
  38.1 7.1 %collective-permute-start = (bf16[2,128,128]{2,1,0:T(8,128)(2,1)S(1)}, bf16[2,128,128]{2,1,0:T(8,128)(2,1)S(1)}, u32[]{:S(2)}, u32[]{:S(2)}) collective-permute-start(bf16[2,128,128]{2,1,0:T(8,128)(2,1)S(1)} %get-tuple-element.314), channel_id=1, source_target_pairs={{0,8},{8,16},{16,24},{24,32},{32,40},{40,48},{48,56},{56,64},{64,7... | collective-permute-start | bytes 196616 | tf_op jit(solution)/shard_map/while/body/eval_jaxpr/ppermute | solution.py:19
  46.0 7.1 %collective-permute-start = (bf16[2,128,128]{2,1,0:T(8,128)(2,1)S(1)}, bf16[2,128,128]{2,1,0:T(8,128)(2,1)S(1)}, u32[]{:S(2)}, u32[]{:S(2)}) collective-permute-start(bf16[2,128,128]{2,1,0:T(8,128)(2,1)S(1)} %get-tuple-element.314), channel_id=1, source_target_pairs={{0,8},{8,16},{16,24},{24,32},{32,40},{40,48},{48,56},{56,64},{64,7... | collective-permute-start | bytes 196616 | tf_op jit(solution)/shard_map/while/body/eval_jaxpr/ppermute | solution.py:19
  53.8 7.1 %collective-permute-start = (bf16[2,128,128]{2,1,0:T(8,128)(2,1)S(1)}, bf16[2,128,128]{2,1,0:T(8,128)(2,1)S(1)}, u32[]{:S(2)}, u32[]{:S(2)}) collective-permute-start(bf16[2,128,128]{2,1,0:T(8,128)(2,1)S(1)} %get-tuple-element.314), channel_id=1, source_target_pairs={{0,8},{8,16},{16,24},{24,32},{32,40},{40,48},{48,56},{56,64},{64,7... | collective-permute-start | bytes 196616 | tf_op jit(solution)/shard_map/while/body/eval_jaxpr/ppermute | solution.py:19
  61.7 7.1 %collective-permute-start = (bf16[2,128,128]{2,1,0:T(8,128)(2,1)S(1)}, bf16[2,128,128]{2,1,0:T(8,128)(2,1)S(1)}, u32[]{:S(2)}, u32[]{:S(2)}) collective-permute-start(bf16[2,128,128]{2,1,0:T(8,128)(2,1)S(1)} %get-tuple-element.314), channel_id=1, source_target_pairs={{0,8},{8,16},{16,24},{24,32},{32,40},{40,48},{48,56},{56,64},{64,7... | collective-permute-start | bytes 196616 | tf_op jit(solution)/shard_map/while/body/eval_jaxpr/ppermute | solution.py:19
  69.5 7.1 %collective-permute-start = (bf16[2,128,128]{2,1,0:T(8,128)(2,1)S(1)}, bf16[2,128,128]{2,1,0:T(8,128)(2,1)S(1)}, u32[]{:S(2)}, u32[]{:S(2)}) collective-permute-start(bf16[2,128,128]{2,1,0:T(8,128)(2,1)S(1)} %get-tuple-element.314), channel_id=1, source_target_pairs={{0,8},{8,16},{16,24},{24,32},{32,40},{40,48},{48,56},{56,64},{64,7... | collective-permute-start | bytes 196616 | tf_op jit(solution)/shard_map/while/body/eval_jaxpr/ppermute | solution.py:19
  77.3 7.1 %collective-permute-start = (bf16[2,128,128]{2,1,0:T(8,128)(2,1)S(1)}, bf16[2,128,128]{2,1,0:T(8,128)(2,1)S(1)}, u32[]{:S(2)}, u32[]{:S(2)}) collective-permute-start(bf16[2,128,128]{2,1,0:T(8,128)(2,1)S(1)} %get-tuple-element.314), channel_id=1, source_target_pairs={{0,8},{8,16},{16,24},{24,32},{32,40},{40,48},{48,56},{56,64},{64,7... | collective-permute-start | bytes 196616 | tf_op jit(solution)/shard_map/while/body/eval_jaxpr/ppermute | solution.py:19
  85.2 7.1 %collective-permute-start = (bf16[2,128,128]{2,1,0:T(8,128)(2,1)S(1)}, bf16[2,128,128]{2,1,0:T(8,128)(2,1)S(1)}, u32[]{:S(2)}, u32[]{:S(2)}) collective-permute-start(bf16[2,128,128]{2,1,0:T(8,128)(2,1)S(1)} %get-tuple-element.314), channel_id=1, source_target_pairs={{0,8},{8,16},{16,24},{24,32},{32,40},{40,48},{48,56},{56,64},{64,7... | collective-permute-start | bytes 196616 | tf_op jit(solution)/shard_map/while/body/eval_jaxpr/ppermute | solution.py:19
  93.0 7.1 %collective-permute-start = (bf16[2,128,128]{2,1,0:T(8,128)(2,1)S(1)}, bf16[2,128,128]{2,1,0:T(8,128)(2,1)S(1)}, u32[]{:S(2)}, u32[]{:S(2)}) collective-permute-start(bf16[2,128,128]{2,1,0:T(8,128)(2,1)S(1)} %get-tuple-element.314), channel_id=1, source_target_pairs={{0,8},{8,16},{16,24},{24,32},{32,40},{40,48},{48,56},{56,64},{64,7... | collective-permute-start | bytes 196616 | tf_op jit(solution)/shard_map/while/body/eval_jaxpr/ppermute | solution.py:19
  100.9 7.8 %collective-permute-start = (bf16[2,128,128]{2,1,0:T(8,128)(2,1)S(1)}, bf16[2,128,128]{2,1,0:T(8,128)(2,1)S(1)}, u32[]{:S(2)}, u32[]{:S(2)}) collective-permute-start(bf16[2,128,128]{2,1,0:T(8,128)(2,1)S(1)} %get-tuple-element.314), channel_id=1, source_target_pairs={{0,8},{8,16},{16,24},{24,32},{32,40},{40,48},{48,56},{56,64},{64,7... | collective-permute-start | bytes 196616 | tf_op jit(solution)/shard_map/while/body/eval_jaxpr/ppermute | solution.py:19
  109.5 8.0 %collective-permute-start = (bf16[2,128,128]{2,1,0:T(8,128)(2,1)S(1)}, bf16[2,128,128]{2,1,0:T(8,128)(2,1)S(1)}, u32[]{:S(2)}, u32[]{:S(2)}) collective-permute-start(bf16[2,128,128]{2,1,0:T(8,128)(2,1)S(1)} %get-tuple-element.314), channel_id=1, source_target_pairs={{0,8},{8,16},{16,24},{24,32},{32,40},{40,48},{48,56},{56,64},{64,7... | collective-permute-start | bytes 196616 | tf_op jit(solution)/shard_map/while/body/eval_jaxpr/ppermute | solution.py:19
  118.2 8.0 %collective-permute-start = (bf16[2,128,128]{2,1,0:T(8,128)(2,1)S(1)}, bf16[2,128,128]{2,1,0:T(8,128)(2,1)S(1)}, u32[]{:S(2)}, u32[]{:S(2)}) collective-permute-start(bf16[2,128,128]{2,1,0:T(8,128)(2,1)S(1)} %get-tuple-element.314), channel_id=1, source_target_pairs={{0,8},{8,16},{16,24},{24,32},{32,40},{40,48},{48,56},{56,64},{64,7... | collective-permute-start | bytes 196616 | tf_op jit(solution)/shard_map/while/body/eval_jaxpr/ppermute | solution.py:19
  127.2 7.0 %copy-start.2 = (s32[128,4]{0,1:T(4,128)S(1)}, s32[128,4]{0,1:T(4,128)}, u32[]{:S(2)}) copy-start(s32[128,4]{0,1:T(4,128)} %param.22) | copy-start | bytes 6148
  127.2 68.2 %copy-start.1 = (bf16[128,768]{1,0:T(8,128)(2,1)S(1)}, bf16[128,768]{1,0:T(8,128)(2,1)}, u32[]{:S(2)}) copy-start(bf16[128,768]{1,0:T(8,128)(2,1)} %param.16) | copy-start | bytes 589828
  127.2 88.1 %copy-start.4 = (f32[768]{0:T(1024)S(1)}, f32[768]{0:T(1024)}, u32[]{:S(2)}) copy-start(f32[768]{0:T(1024)} %param.17) | copy-start | bytes 9220
  134.1 201.9 %all-gather.2.cloned.1.call-start = ((), (), s32[]{:S(2)}) async-start(), calls=%async_computation.5 | async-start | bytes 16711680 | tf_op jit(solution)/shard_map/all_gather | solution.py:112
  231.4 276.7 %reduce-scatter.5.cloned.1.call-start = ((), (), s32[]{:S(2)}) async-start(), calls=%async_computation.6 | async-start | bytes 16711680 | tf_op jit(solution)/shard_map/reduce_scatter | solution.py:118
  555.1 19.1 %all-to-all-start.1 = ((bf16[8,2,30720]{2,1,0:T(2,128)(2,1)}), bf16[8,2,30720]{2,1,0:T(2,128)(2,1)}, u32[]{:S(2)}, u32[]{:S(2)}) async-start(bf16[8,2,30720]{2,1,0:T(2,128)(2,1)} %reshape.277), calls=%async_computation.3 | async-start | bytes 1966080 | tf_op jit(solution)/shard_map/all_to_all | solution.py:125
  559.6 3.1 copy-start.3
  586.5 3.5 copy-start
Sparse Core Ops, SparseCore 0:
  134.2 61.1 reduce-scatter.2
  231.5 104.4 all-gather.1
  372.9 135.1 reduce-scatter.4
where the time goes:
time: 599 us; the launch traced here: 597 us
  waiting for transfers between devices  324 us (54%)
  starting transfers between devices  95.9 us (16%)
  matrix products  56.2 us (9%)
  other arithmetic  41.6 us (7%)
  local copies, waits for them, and re-layouts  33.1 us (6%)
  blocking collectives  32.3 us (5%)
  between operations  13.4 us (2%)
    reduce_scatter x1, waiting for transfers between devices, body(): lax.psum_scatter(result.reshape(lax.axis_size('ctx') * (local_experts * C...  135 us
    all_gather x1, waiting for transfers between devices, body(): lax.all_gather(arrived.reshape(local_experts * CAP, D), 'ctx', axis=0, ti...  104 us
    ppermute x15, starting transfers between devices, shifted(): return lax.ppermute(block, axis, route)  91.4 us
    reduce_scatter x1, waiting for transfers between devices, body(): projected = lax.psum_scatter(term, 'exp', scatter_dimension=1, tiled=True)  61.1 us
    unnamed x1, other arithmetic  34.4 us
    dot_general x1, matrix products, body(): jnp.einsum('necf,efd->necd', act, down_weight, preferred_element_type=jnp...  23.9 us
    psum x1, blocking collectives, body(): lax.psum((jnp.sum(hidden, axis=1), jnp.sum(hidden * hidden, axis=1)), 'exp')  18.7 us
    unnamed x17, local copies, waits for them, and re-layouts  15.2 us
  transfers between devices with their start and end apart: 19, of which 19 were waited for; matrix products, arithmetic and copies ran while one was open for 1% of the time, Pallas kernels for 0%

commit v1 on v0

v1 whole, which is shorter than its diff:
```python
import functools

import jax
import jax.numpy as jnp
from jax import lax
from jax.experimental import pallas as pl
from jax.experimental.pallas import tpu as pltpu
from jax.sharding import PartitionSpec as P

D = 6144
HD = 128
EXPERTS = 8
TOPK = 4
CAP = 80
AUX = 16
TOK = 128
SLICE = 768
SHARDS = 16
UNITS = 336
MAIN = 256
REST = UNITS - MAIN
EPS = 1e-05
F32 = jnp.float32
BF16 = jnp.bfloat16
MIB = 1 << 20


def place(index):
    return index // 4, (index // 2) % 2, index % 2


def route(dy, dz, dc):
    pairs = []
    for index in range(SHARDS):
        y, z, c = place(index)
        pairs.append((index, (((y + dy) % 4) * 2 + (z + dz) % 2) * 2 + (c + dc) % 2))
    return pairs


def send(block, dy=0, dz=0, dc=0):
    return lax.ppermute(block, "ctx", route(dy, dz, dc))


def call(kernel, out_shape, limit, flops, moved, **kwargs):
    return pl.pallas_call(
        kernel,
        out_shape=out_shape,
        compiler_params=pltpu.CompilerParams(vmem_limit_bytes=limit * MIB),
        cost_estimate=pl.CostEstimate(flops=flops, bytes_accessed=moved, transcendentals=0),
        **kwargs,
    )


def shape(dims, dtype=BF16):
    return jax.ShapeDtypeStruct(dims, dtype)


def pieces(value):
    high = value.astype(BF16).astype(F32)
    left = value - high
    mid = left.astype(BF16).astype(F32)
    return high, mid, left - mid


def routing_kernel(ids_ref, scores_ref, placing_ref, high_ref, low_ref):
    ids = ids_ref[...]
    scores = scores_ref[...]
    total = scores[:, 0:1] + scores[:, 1:2] + scores[:, 2:3] + scores[:, 3:4]
    lanes = lax.broadcasted_iota(jnp.int32, (TOK, TOK), 1)
    rows = lax.broadcasted_iota(jnp.int32, (TOK, TOK), 0)
    named = [(lanes == ids[:, k : k + 1]).astype(F32) for k in range(TOPK)]
    member = named[0] + named[1] + named[2] + named[3]
    lower = (lanes < rows).astype(BF16)
    slots = jnp.dot(lower, member.astype(BF16), preferred_element_type=F32)
    wide = lax.broadcasted_iota(jnp.int32, (TOK, EXPERTS * TOK), 1)
    columns = lax.broadcasted_iota(jnp.int32, (TOK, EXPERTS * CAP), 1)
    placed = jnp.zeros((TOK, EXPERTS * TOK), F32)
    shares = jnp.zeros((TOK, EXPERTS * CAP), F32)
    for k in range(TOPK):
        slot = jnp.sum(named[k] * slots, axis=1, keepdims=True).astype(jnp.int32)
        expert = ids[:, k : k + 1]
        placed = placed + (wide == expert * TOK + slot).astype(F32)
        share = scores[:, k : k + 1] / total
        shares = shares + jnp.where(columns == expert * CAP + slot, share, 0.0)
    for e in range(EXPERTS):
        placing_ref[e] = placed[:, e * TOK : (e + 1) * TOK].T.astype(BF16)
    high = shares.astype(BF16)
    high_ref[...] = high
    low_ref[...] = (shares - high.astype(F32)).astype(BF16)


def routing(expert_ids, gate_scores):
    return call(
        routing_kernel,
        (
            shape((EXPERTS, TOK, TOK)),
            shape((TOK, EXPERTS * CAP)),
            shape((TOK, EXPERTS * CAP)),
        ),
        16,
        10**7,
        10**6,
    )(expert_ids, gate_scores)


def attention_kernel(starts_ref, queries_ref, paired_ref, weight_ref, term_ref, held, ready):
    copy = pltpu.make_async_copy(weight_ref, held, ready)
    copy.start()
    keys = paired_ref[:, 0].reshape(SHARDS * TOK, HD)
    values = paired_ref[:, 1].reshape(SHARDS * TOK, HD)
    rows = lax.broadcasted_iota(jnp.int32, (TOK, TOK), 0)
    lanes = lax.broadcasted_iota(jnp.int32, (TOK, TOK), 1)
    ahead = rows - lanes + starts_ref[SHARDS]
    keep = jnp.concatenate([ahead >= starts_ref[b] for b in range(SHARDS)], axis=1)
    heads = []
    for h in range(queries_ref.shape[1] // HD):
        query = queries_ref[:, h * HD : (h + 1) * HD]
        scores = lax.dot_general(
            query, keys, (((1,), (1,)), ((), ())), preferred_element_type=F32
        ) * (HD**-0.5)
        scores = jnp.where(keep, scores, -1e30)
        top = jnp.max(scores, axis=1, keepdims=True)
        expw = jnp.exp(scores - top)
        denom = jnp.sum(expw, axis=1, keepdims=True)
        summed = jnp.dot(expw.astype(BF16), values, preferred_element_type=F32)
        heads.append((summed / denom).astype(BF16))
    attended = jnp.concatenate(heads, axis=1)
    copy.wait()
    for j in range(EXPERTS):
        term_ref[j] = jnp.dot(
            attended, held[:, j * SLICE : (j + 1) * SLICE], preferred_element_type=F32
        ).astype(BF16)


def attention(starts, queries, paired, out_weight):
    return call(
        attention_kernel,
        shape((EXPERTS, TOK, SLICE)),
        48,
        2 * 10**9,
        13 * 10**6,
        in_specs=[
            pl.BlockSpec(memory_space=pltpu.SMEM),
            pl.BlockSpec(memory_space=pltpu.VMEM),
            pl.BlockSpec(memory_space=pltpu.VMEM),
            pl.BlockSpec(memory_space=pl.ANY),
        ],
        out_specs=pl.BlockSpec(memory_space=pltpu.VMEM),
        scratch_shapes=[pltpu.VMEM((SLICE, D), BF16), pltpu.SemaphoreType.DMA],
    )(starts, queries, paired, out_weight)


def dispatch_kernel(terms_ref, residual_ref, gain_ref, placing_ref, hidden_ref, out_ref):
    hidden = residual_ref[...].astype(F32)
    for j in range(EXPERTS):
        hidden = hidden + terms_ref[j].astype(F32)
    hidden_ref[...] = hidden
    mean = jnp.sum(hidden, axis=1, keepdims=True) * (1.0 / SLICE)
    apart = (hidden - mean).astype(BF16)
    lanes = lax.broadcasted_iota(jnp.int32, (TOK, TOK), 1)
    high, mid, low = pieces(mean)
    spread = jnp.where(lanes == 0, high, jnp.where(lanes == 1, mid, jnp.where(lanes == 2, low, 0.0)))
    means = spread.T[:AUX].astype(BF16)
    rows = lax.broadcasted_iota(jnp.int32, (AUX, SLICE), 0)
    high, mid, low = pieces(gain_ref[...])
    gains = jnp.where(rows == 3, high, jnp.where(rows == 4, mid, jnp.where(rows == 5, low, 0.0)))
    for e in range(EXPERTS):
        placing = placing_ref[e]
        out_ref[e, :CAP] = jnp.dot(placing[:CAP], apart, preferred_element_type=F32).astype(BF16)
        sent = lax.dot_general(means, placing, (((1,), (1,)), ((), ())), preferred_element_type=F32)
        out_ref[e, CAP:] = jnp.concatenate(
            [sent + gains[:, :TOK], gains[:, TOK:]], axis=1
        ).astype(BF16)


def dispatch(terms, residual, gain, placing):
    return call(
        dispatch_kernel,
        (shape((TOK, SLICE), F32), shape((EXPERTS, CAP + AUX, SLICE))),
        24,
        2 * 10**8,
        5 * 10**6,
    )(terms, residual, gain, placing)


def norm_kernel(arrived_ref, out_ref):
    rows = lax.broadcasted_iota(jnp.int32, (CAP, TOK), 0)
    lanes = lax.broadcasted_iota(jnp.int32, (CAP, TOK), 1)
    diagonal = (rows == lanes).astype(BF16)
    means = []
    total = jnp.zeros((CAP, 1), F32)
    for j in range(EXPERTS):
        turned = lax.dot_general(
            diagonal, arrived_ref[j, CAP:, :TOK], (((1,), (1,)), ((), ())), preferred_element_type=F32
        )
        means.append(turned[:, 0:1] + turned[:, 1:2] + turned[:, 2:3])
        total = total + SLICE * means[j]
        total = total + jnp.sum(arrived_ref[j, :CAP].astype(F32), axis=1, keepdims=True)
    mean = total / D
    spread = jnp.zeros((CAP, 1), F32)
    for j in range(EXPERTS):
        apart = arrived_ref[j, :CAP].astype(F32) + (means[j] - mean)
        spread = spread + jnp.sum(apart * apart, axis=1, keepdims=True)
    scale = lax.rsqrt(spread / D + EPS)
    for j in range(EXPERTS):
        aux = arrived_ref[j, CAP:].astype(F32)
        gain = aux[3:4] + aux[4:5] + aux[5:6]
        apart = arrived_ref[j, :CAP].astype(F32) + (means[j] - mean)
        out_ref[j] = (apart * scale * gain).astype(BF16)


def norm(arrived):
    return call(norm_kernel, shape((EXPERTS, CAP, SLICE)), 16, 10**7, 2 * 10**6)(arrived)


STEP = 2
STEPS = EXPERTS // STEP


def expert_kernel(parts, *refs):
    count = len(parts)
    xs, refs = refs[:count], refs[count:]
    gate_own, gate_other, up_own, up_other, down_own, down_other = refs[:6]
    outs = refs[6 : 6 + count]
    rows_ref, gate_sum, up_sum, act_ref, gate_rest, up_rest, down_rest = refs[6 + count :]
    step = pl.program_id(0)

    @pl.when(step == 0)
    def _():
        gate_sum[...] = jnp.zeros_like(gate_sum)
        up_sum[...] = jnp.zeros_like(up_sum)
        gate_rest[...] = jnp.zeros_like(gate_rest)
        up_rest[...] = jnp.zeros_like(up_rest)
        down_rest[...] = jnp.zeros_like(down_rest)

    @pl.when(step < STEPS)
    def _():
        for (shard, start, steps), x in zip(parts, xs):

            @pl.when((step >= start) & (step < start + steps))
            def _():
                for k in range(STEP):
                    rows_ref[shard * CAP : (shard + 1) * CAP, k * SLICE : (k + 1) * SLICE] = x[k]

        rows = rows_ref[...]
        for own, other, rest, total in (
            (gate_own, gate_other, gate_rest, gate_sum),
            (up_own, up_other, up_rest, up_sum),
        ):
            rest[:, :REST] = own[0, :, MAIN:]
            rest[:, 128 : 128 + REST] = other[0, :, MAIN:]
            total[:, :MAIN] += jnp.dot(rows, own[0, :, :MAIN], preferred_element_type=F32)
            total[:, MAIN : 2 * MAIN] += jnp.dot(
                rows, other[0, :, :MAIN], preferred_element_type=F32
            )
            total[:, 2 * MAIN :] += jnp.dot(rows, rest[...], preferred_element_type=F32)

    @pl.when(step == STEPS)
    def _():
        gate = gate_sum[...]
        act_ref[...] = (gate / (1.0 + jnp.exp(-gate)) * up_sum[...]).astype(BF16)

    @pl.when(step >= STEPS)
    def _():
        down_rest[:REST] = down_own[0, MAIN:]
        down_rest[128 : 128 + REST] = down_other[0, MAIN:]
        for k in range(STEP):
            cols = slice(k * SLICE, (k + 1) * SLICE)
            result = jnp.dot(act_ref[:, :MAIN], down_own[0, :MAIN, cols], preferred_element_type=F32)
            result += jnp.dot(
                act_ref[:, MAIN : 2 * MAIN], down_other[0, :MAIN, cols], preferred_element_type=F32
            )
            result += jnp.dot(
                act_ref[:, 2 * MAIN :], down_rest[:, cols], preferred_element_type=F32
            )
            result = result.astype(BF16)
            for (shard, start, steps), out in zip(parts, outs):

                @pl.when((step >= STEPS + start) & (step < STEPS + start + steps))
                def _():
                    out[k] = result[shard * CAP : (shard + 1) * CAP]


def expert(shards, weights):
    parts, arrays = [], []
    for number, split in enumerate(shards):
        start = 0
        for array in split:
            steps = array.shape[0] // STEP
            parts.append((number, start, steps))
            arrays.append(array)
            start += steps
    total = CAP * len(shards)
    width = STEP * SLICE

    def rows_spec(part, late):
        _, start, steps = part
        return pl.BlockSpec(
            (STEP, CAP, SLICE),
            lambda i: (jnp.clip(i - start - late, 0, steps - 1), 0, 0),
        )

    across = pl.BlockSpec((1, width, UNITS), lambda i: (0, jnp.minimum(i, STEPS - 1), 0))
    along = pl.BlockSpec((1, UNITS, width), lambda i: (0, 0, jnp.maximum(i - STEPS, 0)))
    outs = call(
        functools.partial(expert_kernel, parts),
        tuple(shape(array.shape) for array in arrays),
        44,
        total * D * 2 * UNITS * 6,
        27 * 10**6,
        grid=(2 * STEPS,),
        in_specs=[rows_spec(part, 0) for part in parts] + [across] * 4 + [along] * 2,
        out_specs=tuple(rows_spec(part, STEPS) for part in parts),
        scratch_shapes=[
            pltpu.VMEM((total, width), BF16),
            pltpu.VMEM((total, 3 * MAIN), F32),
            pltpu.VMEM((total, 3 * MAIN), F32),
            pltpu.VMEM((total, 3 * MAIN), BF16),
            pltpu.VMEM((width, MAIN), BF16),
            pltpu.VMEM((width, MAIN), BF16),
            pltpu.VMEM((MAIN, width), BF16),
        ],
    )(*arrays, *weights)
    results, taken = [], 0
    for split in shards:
        results.append(list(outs[taken : taken + len(split)]))
        taken += len(split)
    return results


def add(*values):
    total = values[0].astype(F32)
    for value in values[1:]:
        total = total + value.astype(F32)
    return total.astype(BF16)


def combine_kernel(hidden_ref, high_ref, low_ref, outputs_ref, mixed_ref):
    outputs = outputs_ref[...].reshape(EXPERTS * CAP, SLICE)
    moe = jnp.dot(high_ref[...], outputs, preferred_element_type=F32)
    moe += jnp.dot(low_ref[...], outputs, preferred_element_type=F32)
    mixed_ref[...] = (hidden_ref[...] + moe).astype(BF16)


def combine(hidden, high, low, outputs):
    return call(combine_kernel, shape((TOK, SLICE)), 16, 3 * 10**8, 2 * 10**6)(
        hidden, high, low, outputs
    )


def body(
    queries,
    keys,
    values,
    residual,
    ln_gain,
    out_weight,
    gate_weight,
    up_weight,
    down_weight,
    expert_ids,
    gate_scores,
):
    ctx = lax.axis_index("ctx")
    own = jnp.stack((keys, values))[None]
    near = jnp.concatenate([own, send(own, dz=1)])
    near = jnp.concatenate([near, send(near, dy=1), send(near, dy=-1), send(near, dy=2)])
    paired = jnp.concatenate([near, send(near, dc=1)])
    y, z, c = ctx // 4, (ctx // 2) % 2, ctx % 2
    starts = [
        ((((y - dy) % 4) * 2 + (z + dz) % 2) * 2 + (c + dc) % 2) * TOK
        for dc in (0, 1)
        for dy in (0, 1, -1, 2)
        for dz in (0, 1)
    ]
    starts = jnp.stack(starts + [ctx * TOK]).astype(jnp.int32)
    placing, high, low = routing(expert_ids, gate_scores)
    weights = []
    for weight in (gate_weight, up_weight, down_weight):
        weights += [weight, send(weight, dc=1)]

    term = attention(starts, queries, paired, out_weight)
    terms = lax.all_to_all(term, "exp", 0, 0, tiled=True)
    hidden, outgoing = dispatch(terms, residual, ln_gain[None], placing)
    arrived = lax.all_to_all(outgoing, "exp", 0, 0, tiled=True)
    mine = norm(arrived)

    half = EXPERTS // 2
    back, ahead, across = send(mine, dy=1), send(mine, dy=-1), send(mine, dz=1)
    across_back, across_ahead = send(across, dy=1), send(across, dy=-1)
    far = [send(back[:half], dy=1), send(ahead[half:], dy=-1)]
    across_far = [send(across_back[:half], dy=1), send(across_ahead[half:], dy=-1)]
    first = expert([[mine], [across], [back], [ahead]], weights)
    second = expert([[across_back], [across_ahead], far, across_far], weights)
    part = [first[0][0], first[2][0], first[3][0], second[2]]
    across_part = [first[1][0], second[0][0], second[1][0], second[3]]

    def ring(part):
        mine, back, ahead, far = part
        low_half, high_half = send(far[0], dy=1), send(far[1], dy=-1)
        ahead = jnp.concatenate([add(ahead[:half], low_half), ahead[half:]])
        back = jnp.concatenate([back[:half], add(back[half:], high_half)])
        return mine, send(ahead, dy=1), send(back, dy=-1)

    across_sum = send(add(*ring(across_part)), dz=1)
    result = add(across_sum, *ring(part))
    outputs = lax.all_to_all(result, "exp", 0, 0, tiled=True)
    return combine(hidden, high, low, outputs)


def solution(mesh):
    return jax.shard_map(
        body,
        mesh=mesh,
        in_specs=(
            P("ctx", "exp"),
            P("ctx", "exp"),
            P("ctx", "exp"),
            P("ctx", "exp"),
            P("exp"),
            P("exp", None),
            P("exp", None, "ctx"),
            P("exp", None, "ctx"),
            P("exp", "ctx", None),
            P("ctx", None),
            P("ctx", None),
        ),
        out_specs=P("ctx", "exp"),
        check_vma=False,
    )
```

time: 599 us -> 290 us (0.48)
  waiting for transfers between devices: 324 us -> 128 us
  matrix products: 56.2 us -> 0 us
  Pallas kernels: 0 us -> 55.7 us
  starting transfers between devices: 95.9 us -> 51 us
  other arithmetic: 41.6 us -> 3.27 us
  blocking collectives: 32.3 us -> 15.2 us
  between operations: 13.4 us -> 0.54 us
    reduce_scatter x2 -> x0, waiting for transfers between devices: 196 us -> none  [the longest x1 135 us: body(): lax.psum_scatter(result.reshape(lax.axis_size('ctx') * (local_experts * C...]
    all_gather x1 -> x0, waiting for transfers between devices: 104 us -> none  [body(): lax.all_gather(arrived.reshape(local_experts * CAP, D), 'ctx', axis=0, ti...]
    ppermute x15 -> x26, waiting for transfers between devices: 11.5 us -> 92.6 us  [send(): return lax.ppermute(block, 'ctx', route(dy, dz, dc))]
    dot_general x37 -> x0, matrix products: 56.2 us -> none  [the longest x1 23.9 us: body(): jnp.einsum('necf,efd->necd', act, down_weight, preferred_element_type=jnp...]
    pallas_call x0 -> x7, Pallas kernels: none -> 55.7 us  [the longest x2 39.4 us: expert(): call(functools.partial(expert_kernel, parts), tuple((shape(array.shape) f...]
    ppermute x15 -> x26, starting transfers between devices: 91.4 us -> 42 us  [send(): return lax.ppermute(block, 'ctx', route(dy, dz, dc))]
    unnamed x1, other arithmetic: 34.4 us -> 0.79 us
    all_to_all x1 -> x2, waiting for transfers between devices: 11.3 us -> 35.2 us  [the longest x1 18.2 us: body(): terms = lax.all_to_all(term, 'exp', 0, 0, tiled=True)]
  transfers between devices with their start and end apart: 19 -> 28, of which waited for: 19 -> 16; matrix products, arithmetic and copies ran while one was open for 1% -> 11% of each run, Pallas kernels for 0% -> 8%
where the time goes in v1:
time: 290 us; the launch traced here: 289 us
  waiting for transfers between devices  128 us (44%)
  Pallas kernels  55.7 us (19%)
  starting transfers between devices  51 us (18%)
  local copies, waits for them, and re-layouts  35.5 us (12%)
  blocking collectives  15.2 us (5%)
  other arithmetic  3.27 us (1%)
    ppermute x26, waiting for transfers between devices, send(): return lax.ppermute(block, 'ctx', route(dy, dz, dc))  92.6 us
    ppermute x26, starting transfers between devices, send(): return lax.ppermute(block, 'ctx', route(dy, dz, dc))  42 us
    pallas_call x2, Pallas kernels, expert(): call(functools.partial(expert_kernel, parts), tuple((shape(array.shape) f...  39.4 us
    unnamed x37, local copies, waits for them, and re-layouts  19 us
    all_to_all x1, waiting for transfers between devices, body(): terms = lax.all_to_all(term, 'exp', 0, 0, tiled=True)  18.2 us
    all_to_all x1, waiting for transfers between devices, body(): arrived = lax.all_to_all(outgoing, 'exp', 0, 0, tiled=True)  17 us
    all_to_all x1, blocking collectives, body(): outputs = lax.all_to_all(result, 'exp', 0, 0, tiled=True)  15.2 us
    ppermute x2, local copies, waits for them, and re-layouts, send(): return lax.ppermute(block, 'ctx', route(dy, dz, dc))  12.9 us
  transfers between devices with their start and end apart: 28, of which 16 were waited for; matrix products, arithmetic and copies ran while one was open for 11% of the time, Pallas kernels for 8%

profile of v1, /device:TPU:0, one launch (start us, length us, event | category | flops | bytes accessed | tf_op | source)
XLA Modules:
  0.0 289.0 jit_solution(10435169034952562255)
XLA Ops:
  0.8 4.0 %collective-permute-start = (bf16[1,2,128,128]{3,2,1,0:T(8,128)(2,1)S(1)}, bf16[1,2,128,128]{3,2,1,0:T(8,128)(2,1)S(1)}, u32[]{:S(2)}, u32[]{:S(2)}) collective-permute-start(bf16[1,2,128,128]{3,2,1,0:T(8,128)(2,1)S(1)} %maximum_bitcast_fusion), channel_id=1, source_target_pairs={{0,16},{8,24},{16,0},{24,8},{32,48},{40,56},{48,32},{56,40},{64,80... | collective-permute-start | bytes 196616 | tf_op jit(solution)/shard_map/ppermute | solution.py:41
  9.6 3.0 %collective-permute-start.3 = (bf16[2,2,128,128]{3,2,1,0:T(8,128)(2,1)S(1)}, bf16[2,2,128,128]{3,2,1,0:T(8,128)(2,1)S(1)}, u32[]{:S(2)}, u32[]{:S(2)}) collective-permute-start(bf16[2,2,128,128]{3,2,1,0:T(8,128)(2,1)S(1)} %pad_maximum_fusion.4), channel_id=1, source_target_pairs={{0,64},{8,72},{16,80},{24,88},{32,96},{40,104},{48,112},{56,120},{... | collective-permute-start | bytes 393224 | tf_op jit(solution)/shard_map/ppermute | solution.py:41
  14.8 2.9 %collective-permute-done.2 = bf16[2,2,128,128]{3,2,1,0:T(8,128)(2,1)S(1)} collective-permute-done((bf16[2,2,128,128]{3,2,1,0:T(8,128)(2,1)S(1)}, bf16[2,2,128,128]{3,2,1,0:T(8,128)(2,1)S(1)}, u32[]{:S(2)}, u32[]{:S(2)}) %collective-permute-start.2) | collective-permute-done | bytes 131104 | tf_op jit(solution)/shard_map/ppermute | solution.py:41
  19.9 10.0 %shard_map.109 = bf16[8,128,768]{2,1,0:T(8,128)(2,1)} custom-call(s32[17]{0:T(128)S(1)} %stack.80.starts_ref, bf16[128,768]{1,0:T(8,128)(2,1)S(1)} %copy-done.7, bf16[16,2,128,128]{3,2,1,0:T(8,128)(2,1)S(1)} %constant_dynamic-update-slice_fusion.5.paired_ref, bf16[768,6144]{1,0:T(8,128)(2,1)} %weight_ref.1), custom_call_target="tpu_custom_call" | custom-call | flops 2000000000 | bytes 13000000 | tf_op jit(solution)/shard_map/pallas_call | solution.py:136
  30.0 5.2 %all-to-all-start = ((bf16[8,128,768]{2,1,0:T(8,128)(2,1)}), bf16[8,128,768]{2,1,0:T(8,128)(2,1)S(1)}, u32[]{:S(2)}, u32[]{:S(2)}) async-start(bf16[8,128,768]{2,1,0:T(8,128)(2,1)} %shard_map.109), calls=%async_computation | async-start | bytes 3145728 | tf_op jit(solution)/shard_map/all_to_all | solution.py:383
  38.6 18.2 %all-to-all-done.terms_ref = bf16[8,128,768]{2,1,0:T(8,128)(2,1)S(1)} async-done(((bf16[8,128,768]{2,1,0:T(8,128)(2,1)}), bf16[8,128,768]{2,1,0:T(8,128)(2,1)S(1)}, u32[]{:S(2)}, u32[]{:S(2)}) %all-to-all-start) | async-done | bytes 1572896 | tf_op jit(solution)/shard_map/all_to_all | solution.py:383
  58.7 3.8 %all-to-all-start.1 = ((bf16[8,96,768]{2,1,0:T(8,128)(2,1)}), bf16[8,96,768]{2,1,0:T(8,128)(2,1)S(1)}, u32[]{:S(2)}, u32[]{:S(2)}) async-start(bf16[8,96,768]{2,1,0:T(8,128)(2,1)} %get-tuple-element.24), calls=%async_computation.1 | async-start | bytes 2359296 | tf_op jit(solution)/shard_map/all_to_all | solution.py:385
  62.5 17.0 %all-to-all-done.1.arrived_ref = bf16[8,96,768]{2,1,0:T(8,128)(2,1)S(1)} async-done(((bf16[8,96,768]{2,1,0:T(8,128)(2,1)}), bf16[8,96,768]{2,1,0:T(8,128)(2,1)S(1)}, u32[]{:S(2)}, u32[]{:S(2)}) %all-to-all-start.1) | async-done | bytes 1179680 | tf_op jit(solution)/shard_map/all_to_all | solution.py:385
  84.2 3.6 %collective-permute-start.5 = (bf16[8,80,768]{2,1,0:T(8,128)(2,1)S(1)}, bf16[8,80,768]{2,1,0:T(8,128)(2,1)S(1)}, u32[]{:S(2)}, u32[]{:S(2)}) collective-permute-start(bf16[8,80,768]{2,1,0:T(8,128)(2,1)S(1)} %shard_map.112.refs_0_), channel_id=1, source_target_pairs={{0,16},{8,24},{16,0},{24,8},{32,48},{40,56},{48,32},{56,40},{64,80... | collective-permute-start | bytes 2949128 | tf_op jit(solution)/shard_map/ppermute | solution.py:41
  87.8 17.3 %collective-permute-done.7.refs_3_ = bf16[8,80,768]{2,1,0:T(8,128)(2,1)S(1)} collective-permute-done((bf16[8,80,768]{2,1,0:T(8,128)(2,1)S(1)}, bf16[8,80,768]{2,1,0:T(8,128)(2,1)S(1)}, u32[]{:S(2)}, u32[]{:S(2)}) %collective-permute-start.7) | collective-permute-done | bytes 983072 | tf_op jit(solution)/shard_map/ppermute | solution.py:41
  105.9 3.1 %collective-permute-done.5.refs_1_ = bf16[8,80,768]{2,1,0:T(8,128)(2,1)S(1)} collective-permute-done((bf16[8,80,768]{2,1,0:T(8,128)(2,1)S(1)}, bf16[8,80,768]{2,1,0:T(8,128)(2,1)S(1)}, u32[]{:S(2)}, u32[]{:S(2)}) %collective-permute-start.5) | collective-permute-done | bytes 983072 | tf_op jit(solution)/shard_map/ppermute | solution.py:41
  109.5 19.9 %collective-permute-done.6.refs_2_ = bf16[8,80,768]{2,1,0:T(8,128)(2,1)S(1)} collective-permute-done((bf16[8,80,768]{2,1,0:T(8,128)(2,1)S(1)}, bf16[8,80,768]{2,1,0:T(8,128)(2,1)S(1)}, u32[]{:S(2)}, u32[]{:S(2)}) %collective-permute-start.6) | collective-permute-done | bytes 983072 | tf_op jit(solution)/shard_map/ppermute | solution.py:41
  131.5 2.8 collective-permute-start.14
  136.1 16.3 %collective-permute-done.11.refs_0_ = bf16[8,80,768]{2,1,0:T(8,128)(2,1)S(1)} collective-permute-done((bf16[8,80,768]{2,1,0:T(8,128)(2,1)S(1)}, bf16[8,80,768]{2,1,0:T(8,128)(2,1)S(1)}, u32[]{:S(2)}, u32[]{:S(2)}) %collective-permute-start.11) | collective-permute-done | bytes 983072 | tf_op jit(solution)/shard_map/ppermute | solution.py:41
  154.2 3.2 %collective-permute-start.16 = (bf16[4,80,768]{2,1,0:T(8,128)(2,1)}, bf16[4,80,768]{2,1,0:T(8,128)(2,1)}, u32[]{:S(2)}, u32[]{:S(2)}) collective-permute-start(bf16[4,80,768]{2,1,0:T(8,128)(2,1)} %slice.51), channel_id=1, source_target_pairs={{0,96},{8,104},{16,112},{24,120},{32,0},{40,8},{48,16},{56,24},{64... | collective-permute-start | bytes 1474568 | tf_op jit(solution)/shard_map/ppermute | solution.py:41
  157.4 6.5 %copy.22.refs_4_.refs_6_ = bf16[1,6144,336]{2,1,0:T(8,128)(2,1)} copy(bf16[1,6144,336]{1,2,0:T(8,128)(2,1)} %param.17) | data formatting | bytes 8257536 | tf_op args[6]
  163.9 6.5 %copy.24.refs_6_.refs_8_ = bf16[1,6144,336]{2,1,0:T(8,128)(2,1)} copy(bf16[1,6144,336]{1,2,0:T(8,128)(2,1)} %param.18) | data formatting | bytes 8257536 | tf_op args[7]
  170.4 6.4 %copy.23.refs_5_.refs_7_ = bf16[1,6144,336]{2,1,0:T(8,128)(2,1)} copy(bf16[1,6144,336]{1,2,0:T(8,128)(2,1)} %collective-permute-done.8) | data formatting | bytes 8257536 | tf_op jit(solution)/shard_map/ppermute | solution.py:41
  176.8 6.5 %copy.25.refs_7_.refs_9_ = bf16[1,6144,336]{2,1,0:T(8,128)(2,1)} copy(bf16[1,6144,336]{1,2,0:T(8,128)(2,1)} %collective-permute-done.9) | data formatting | bytes 8257536 | tf_op jit(solution)/shard_map/ppermute | solution.py:41
  185.7 20.1 %shard_map.114 = (bf16[8,80,768]{2,1,0:T(8,128)(2,1)S(1)}, bf16[8,80,768]{2,1,0:T(8,128)(2,1)S(1)}, bf16[4,80,768]{2,1,0:T(8,128)(2,1)S(1)}, bf16[4,80,768]{2,1,...) custom-call(bf16[8,80,768]{2,1,0:T(8,128)(2,1)S(1)} %copy-done.3, ...), custom_call_target="tpu_custom_call" | custom-call | flops 7927234560 | bytes 27000000 | tf_op jit(solution)/shard_map/pallas_call | solution.py:305
  205.8 3.3 %collective-permute-start.19 = (bf16[4,80,768]{2,1,0:T(8,128)(2,1)S(1)}, bf16[4,80,768]{2,1,0:T(8,128)(2,1)S(1)}, u32[]{:S(2)}, u32[]{:S(2)}) collective-permute-start(bf16[4,80,768]{2,1,0:T(8,128)(2,1)S(1)} %get-tuple-element.29), channel_id=1, source_target_pairs={{0,96},{8,104},{16,112},{24,120},{32,0},{40,8},{48,16},{56,24},{64... | collective-permute-start | bytes 1474568 | tf_op jit(solution)/shard_map/ppermute | solution.py:41
  209.2 3.3 %collective-permute-start.24 = (bf16[4,80,768]{2,1,0:T(8,128)(2,1)S(1)}, bf16[4,80,768]{2,1,0:T(8,128)(2,1)S(1)}, u32[]{:S(2)}, u32[]{:S(2)}) collective-permute-start(bf16[4,80,768]{2,1,0:T(8,128)(2,1)S(1)} %get-tuple-element.34), channel_id=1, source_target_pairs={{0,96},{8,104},{16,112},{24,120},{32,0},{40,8},{48,16},{56,24},{64... | collective-permute-start | bytes 1474568 | tf_op jit(solution)/shard_map/ppermute | solution.py:41
  212.5 8.2 %collective-permute-done.19 = bf16[4,80,768]{2,1,0:T(8,128)(2,1)S(1)} collective-permute-done((bf16[4,80,768]{2,1,0:T(8,128)(2,1)S(1)}, bf16[4,80,768]{2,1,0:T(8,128)(2,1)S(1)}, u32[]{:S(2)}, u32[]{:S(2)}) %collective-permute-start.19) | collective-permute-done | bytes 491552 | tf_op jit(solution)/shard_map/ppermute | solution.py:41
  221.0 3.8 %collective-permute-start.20 = (bf16[8,80,768]{2,1,0:T(8,128)(2,1)S(1)}, bf16[8,80,768]{2,1,0:T(8,128)(2,1)S(1)}, u32[]{:S(2)}, u32[]{:S(2)}) collective-permute-start(bf16[8,80,768]{2,1,0:T(8,128)(2,1)S(1)} %pad_maximum_fusion.1), channel_id=1, source_target_pairs={{0,96},{8,104},{16,112},{24,120},{32,0},{40,8},{48,16},{56,24},{64... | collective-permute-start | bytes 2949128 | tf_op jit(solution)/shard_map/ppermute | solution.py:41
  225.3 19.3 %shard_map.113 = (bf16[8,80,768]{2,1,0:T(8,128)(2,1)S(1)}, bf16[8,80,768]{2,1,0:T(8,128)(2,1)S(1)}, bf16[8,80,768]{2,1,0:T(8,128)(2,1)S(1)}, bf16[8,80,768]{2,1,0:T(8,128)(2,1)S(1)}) custom-call(bf16[8,80,768]{2,1,0:T(8,128)(2,1)S(1)} %shard_map.112.refs_0_, bf16[8,80,768]{2,1,0:T(8,128)(2,1)S(1)} %copy-done.5, ...), custom_call_target="tpu_custom_call" | custom-call | flops 7927234560 | bytes 27000000 | tf_op jit(solution)/shard_map/pallas_call | solution.py:305
  244.9 3.3 %collective-permute-start.25 = (bf16[8,80,768]{2,1,0:T(8,128)(2,1)S(1)}, bf16[8,80,768]{2,1,0:T(8,128)(2,1)S(1)}, u32[]{:S(2)}, u32[]{:S(2)}) collective-permute-start(bf16[8,80,768]{2,1,0:T(8,128)(2,1)S(1)} %pad_maximum_fusion.3), channel_id=1, source_target_pairs={{0,96},{8,104},{16,112},{24,120},{32,0},{40,8},{48,16},{56,24},{64... | collective-permute-start | bytes 2949128 | tf_op jit(solution)/shard_map/ppermute | solution.py:41
  248.5 3.9 %collective-permute-done.20 = bf16[8,80,768]{2,1,0:T(8,128)(2,1)S(1)} collective-permute-done((bf16[8,80,768]{2,1,0:T(8,128)(2,1)S(1)}, bf16[8,80,768]{2,1,0:T(8,128)(2,1)S(1)}, u32[]{:S(2)}, u32[]{:S(2)}) %collective-permute-start.20) | collective-permute-done | bytes 983072 | tf_op jit(solution)/shard_map/ppermute | solution.py:41
  252.4 3.7 %collective-permute-done.18 = bf16[8,80,768]{2,1,0:T(8,128)(2,1)S(1)} collective-permute-done((bf16[8,80,768]{2,1,0:T(8,128)(2,1)S(1)}, bf16[8,80,768]{2,1,0:T(8,128)(2,1)S(1)}, u32[]{:S(2)}, u32[]{:S(2)}) %collective-permute-start.18) | collective-permute-done | bytes 983072 | tf_op jit(solution)/shard_map/ppermute | solution.py:41
  256.4 3.7 %collective-permute-start.21 = (bf16[8,80,768]{2,1,0:T(8,128)(2,1)S(1)}, bf16[8,80,768]{2,1,0:T(8,128)(2,1)S(1)}, u32[]{:S(2)}, u32[]{:S(2)}) collective-permute-start(bf16[8,80,768]{2,1,0:T(8,128)(2,1)S(1)} %add_convert_fusion.1), channel_id=1, source_target_pairs={{0,16},{8,24},{16,0},{24,8},{32,48},{40,56},{48,32},{56,40},{64,80... | collective-permute-start | bytes 2949128 | tf_op jit(solution)/shard_map/ppermute | solution.py:41
  260.1 8.7 %collective-permute-done.25 = bf16[8,80,768]{2,1,0:T(8,128)(2,1)S(1)} collective-permute-done((bf16[8,80,768]{2,1,0:T(8,128)(2,1)S(1)}, bf16[8,80,768]{2,1,0:T(8,128)(2,1)S(1)}, u32[]{:S(2)}, u32[]{:S(2)}) %collective-permute-start.25) | collective-permute-done | bytes 983072 | tf_op jit(solution)/shard_map/ppermute | solution.py:41
  268.7 3.4 %collective-permute-done.23 = bf16[8,80,768]{2,1,0:T(8,128)(2,1)S(1)} collective-permute-done((bf16[8,80,768]{2,1,0:T(8,128)(2,1)S(1)}, bf16[8,80,768]{2,1,0:T(8,128)(2,1)S(1)}, u32[]{:S(2)}, u32[]{:S(2)}) %collective-permute-start.23) | collective-permute-done | bytes 983072 | tf_op jit(solution)/shard_map/ppermute | solution.py:41
  272.7 15.2 %all_to_all.15.outputs_ref = bf16[8,80,768]{2,1,0:T(8,128)(2,1)S(1)} all-to-all(bf16[8,80,768]{2,1,0:T(8,128)(2,1)S(1)} %add_convert_fusion), channel_id=1, replica_groups=mesh['ctx'=16,'exp'=8] {'exp'}, dimensions={0} | all-to-all | bytes 1966080 | tf_op jit(solution)/shard_map/all_to_all | solution.py:407
  (96 shorter events, 32.6 us)
Async XLA Ops:
  0.0 19.9 %copy-start.7 = (bf16[128,768]{1,0:T(8,128)(2,1)S(1)}, bf16[128,768]{1,0:T(8,128)(2,1)}, u32[]{:S(2)}) copy-start(bf16[128,768]{1,0:T(8,128)(2,1)} %queries_ref.1) | copy-start | bytes 589828
  0.8 6.3 %collective-permute-start = (bf16[1,2,128,128]{3,2,1,0:T(8,128)(2,1)S(1)}, bf16[1,2,128,128]{3,2,1,0:T(8,128)(2,1)S(1)}, u32[]{:S(2)}, u32[]{:S(2)}) collective-permute-start(bf16[1,2,128,128]{3,2,1,0:T(8,128)(2,1)S(1)} %maximum_bitcast_fusion), channel_id=1, source_target_pairs={{0,16},{8,24},{16,0},{24,8},{32,48},{40,56},{48,32},{56,40},{64,80... | collective-permute-start | bytes 196616 | tf_op jit(solution)/shard_map/ppermute | solution.py:41
  7.1 7.7 %collective-permute-start.1 = (bf16[2,2,128,128]{3,2,1,0:T(8,128)(2,1)S(1)}, bf16[2,2,128,128]{3,2,1,0:T(8,128)(2,1)S(1)}, u32[]{:S(2)}, u32[]{:S(2)}) collective-permute-start(bf16[2,2,128,128]{3,2,1,0:T(8,128)(2,1)S(1)} %pad_maximum_fusion.4), channel_id=1, source_target_pairs={{0,32},{8,40},{16,48},{24,56},{32,64},{40,72},{48,80},{56,88},{64,... | collective-permute-start | bytes 393224 | tf_op jit(solution)/shard_map/ppermute | solution.py:41
  9.6 8.3 %collective-permute-start.3 = (bf16[2,2,128,128]{3,2,1,0:T(8,128)(2,1)S(1)}, bf16[2,2,128,128]{3,2,1,0:T(8,128)(2,1)S(1)}, u32[]{:S(2)}, u32[]{:S(2)}) collective-permute-start(bf16[2,2,128,128]{3,2,1,0:T(8,128)(2,1)S(1)} %pad_maximum_fusion.4), channel_id=1, source_target_pairs={{0,64},{8,72},{16,80},{24,88},{32,96},{40,104},{48,112},{56,120},{... | collective-permute-start | bytes 393224 | tf_op jit(solution)/shard_map/ppermute | solution.py:41
  12.5 5.2 %collective-permute-start.2 = (bf16[2,2,128,128]{3,2,1,0:T(8,128)(2,1)S(1)}, bf16[2,2,128,128]{3,2,1,0:T(8,128)(2,1)S(1)}, u32[]{:S(2)}, u32[]{:S(2)}) collective-permute-start(bf16[2,2,128,128]{3,2,1,0:T(8,128)(2,1)S(1)} %pad_maximum_fusion.4), channel_id=1, source_target_pairs={{0,96},{8,104},{16,112},{24,120},{32,0},{40,8},{48,16},{56,24},{64... | collective-permute-start | bytes 393224 | tf_op jit(solution)/shard_map/ppermute | solution.py:41
  17.9 2.0 collective-permute-start.4
  30.0 26.8 %copy-start.6 = (bf16[128,768]{1,0:T(8,128)(2,1)S(1)}, bf16[128,768]{1,0:T(8,128)(2,1)}, u32[]{:S(2)}) copy-start(bf16[128,768]{1,0:T(8,128)(2,1)} %residual_ref.1) | copy-start | bytes 589828
  30.0 26.8 %all-to-all-start = ((bf16[8,128,768]{2,1,0:T(8,128)(2,1)}), bf16[8,128,768]{2,1,0:T(8,128)(2,1)S(1)}, u32[]{:S(2)}, u32[]{:S(2)}) async-start(bf16[8,128,768]{2,1,0:T(8,128)(2,1)} %shard_map.109), calls=%async_computation | async-start | bytes 3145728 | tf_op jit(solution)/shard_map/all_to_all | solution.py:383
  35.2 119.0 %collective-permute-start.8 = (bf16[1,6144,336]{1,2,0:T(8,128)(2,1)}, bf16[1,6144,336]{1,2,0:T(8,128)(2,1)}, u32[]{:S(2)}, u32[]{:S(2)}) collective-permute-start(bf16[1,6144,336]{1,2,0:T(8,128)(2,1)} %param.17), channel_id=1, source_target_pairs={{0,8},{8,0},{16,24},{24,16},{32,40},{40,32},{48,56},{56,48},{64,72... | collective-permute-start | bytes 12386312 | tf_op jit(solution)/shard_map/ppermute | solution.py:41
  35.2 122.2 %collective-permute-start.9 = (bf16[1,6144,336]{1,2,0:T(8,128)(2,1)}, bf16[1,6144,336]{1,2,0:T(8,128)(2,1)}, u32[]{:S(2)}, u32[]{:S(2)}) collective-permute-start(bf16[1,6144,336]{1,2,0:T(8,128)(2,1)} %param.18), channel_id=1, source_target_pairs={{0,8},{8,0},{16,24},{24,16},{32,40},{40,32},{48,56},{56,48},{64,72... | collective-permute-start | bytes 12386312 | tf_op jit(solution)/shard_map/ppermute | solution.py:41
  58.7 20.8 %all-to-all-start.1 = ((bf16[8,96,768]{2,1,0:T(8,128)(2,1)}), bf16[8,96,768]{2,1,0:T(8,128)(2,1)S(1)}, u32[]{:S(2)}, u32[]{:S(2)}) async-start(bf16[8,96,768]{2,1,0:T(8,128)(2,1)} %get-tuple-element.24), calls=%async_computation.1 | async-start | bytes 2359296 | tf_op jit(solution)/shard_map/all_to_all | solution.py:385
  62.5 120.8 %collective-permute-start.10 = (bf16[1,336,6144]{2,1,0:T(8,128)(2,1)}, bf16[1,336,6144]{2,1,0:T(8,128)(2,1)}, u32[]{:S(2)}, u32[]{:S(2)}) collective-permute-start(bf16[1,336,6144]{2,1,0:T(8,128)(2,1)} %refs_10_.1), channel_id=1, source_target_pairs={{0,8},{8,0},{16,24},{24,16},{32,40},{40,32},{48,56},{56,48},{64,72... | collective-permute-start | bytes 12386312 | tf_op jit(solution)/shard_map/ppermute | solution.py:41
  81.5 23.5 %collective-permute-start.7 = (bf16[8,80,768]{2,1,0:T(8,128)(2,1)S(1)}, bf16[8,80,768]{2,1,0:T(8,128)(2,1)S(1)}, u32[]{:S(2)}, u32[]{:S(2)}) collective-permute-start(bf16[8,80,768]{2,1,0:T(8,128)(2,1)S(1)} %shard_map.112.refs_0_), channel_id=1, source_target_pairs={{0,96},{8,104},{16,112},{24,120},{32,0},{40,8},{48,16},{56,24},{64... | collective-permute-start | bytes 2949128 | tf_op jit(solution)/shard_map/ppermute | solution.py:41
  84.2 24.9 %collective-permute-start.5 = (bf16[8,80,768]{2,1,0:T(8,128)(2,1)S(1)}, bf16[8,80,768]{2,1,0:T(8,128)(2,1)S(1)}, u32[]{:S(2)}, u32[]{:S(2)}) collective-permute-start(bf16[8,80,768]{2,1,0:T(8,128)(2,1)S(1)} %shard_map.112.refs_0_), channel_id=1, source_target_pairs={{0,16},{8,24},{16,0},{24,8},{32,48},{40,56},{48,32},{56,40},{64,80... | collective-permute-start | bytes 2949128 | tf_op jit(solution)/shard_map/ppermute | solution.py:41
  105.0 24.4 %collective-permute-start.6 = (bf16[8,80,768]{2,1,0:T(8,128)(2,1)S(1)}, bf16[8,80,768]{2,1,0:T(8,128)(2,1)S(1)}, u32[]{:S(2)}, u32[]{:S(2)}) collective-permute-start(bf16[8,80,768]{2,1,0:T(8,128)(2,1)S(1)} %shard_map.112.refs_0_), channel_id=1, source_target_pairs={{0,32},{8,40},{16,48},{24,56},{32,64},{40,72},{48,80},{56,88},{64,... | collective-permute-start | bytes 2949128 | tf_op jit(solution)/shard_map/ppermute | solution.py:41
  109.1 44.2 %copy-start.4 = (bf16[8,80,768]{2,1,0:T(8,128)(2,1)}, bf16[8,80,768]{2,1,0:T(8,128)(2,1)S(1)}, u32[]{:S(2)}) copy-start(bf16[8,80,768]{2,1,0:T(8,128)(2,1)S(1)} %collective-permute-done.5.refs_1_) | copy-start | bytes 2949124
  109.1 22.4 %collective-permute-start.12 = (bf16[8,80,768]{2,1,0:T(8,128)(2,1)S(1)}, bf16[8,80,768]{2,1,0:T(8,128)(2,1)S(1)}, u32[]{:S(2)}, u32[]{:S(2)}) collective-permute-start(bf16[8,80,768]{2,1,0:T(8,128)(2,1)S(1)} %collective-permute-done.5.refs_1_), channel_id=1, source_target_pairs={{0,96},{8,104},{16,112},{24,120},{32,0},{40,8},{48,16},{56,24},{64... | collective-permute-start | bytes 2949128 | tf_op jit(solution)/shard_map/ppermute | solution.py:41
  129.4 23.0 %collective-permute-start.11 = (bf16[8,80,768]{2,1,0:T(8,128)(2,1)S(1)}, bf16[8,80,768]{2,1,0:T(8,128)(2,1)S(1)}, u32[]{:S(2)}, u32[]{:S(2)}) collective-permute-start(bf16[8,80,768]{2,1,0:T(8,128)(2,1)S(1)} %collective-permute-done.5.refs_1_), channel_id=1, source_target_pairs={{0,32},{8,40},{16,48},{24,56},{32,64},{40,72},{48,80},{56,88},{64,... | collective-permute-start | bytes 2949128 | tf_op jit(solution)/shard_map/ppermute | solution.py:41
  131.5 51.8 %collective-permute-start.14 = (bf16[4,80,768]{2,1,0:T(8,128)(2,1)}, bf16[4,80,768]{2,1,0:T(8,128)(2,1)}, u32[]{:S(2)}, u32[]{:S(2)}) collective-permute-start(bf16[4,80,768]{2,1,0:T(8,128)(2,1)} %slice.49), channel_id=1, source_target_pairs={{0,96},{8,104},{16,112},{24,120},{32,0},{40,8},{48,16},{56,24},{64... | collective-permute-start | bytes 1474568 | tf_op jit(solution)/shard_map/ppermute | solution.py:41
  152.4 30.8 %collective-permute-start.13 = (bf16[4,80,768]{2,1,0:T(8,128)(2,1)}, bf16[4,80,768]{2,1,0:T(8,128)(2,1)}, u32[]{:S(2)}, u32[]{:S(2)}) collective-permute-start(bf16[4,80,768]{2,1,0:T(8,128)(2,1)} %slice.48), channel_id=1, source_target_pairs={{0,32},{8,40},{16,48},{24,56},{32,64},{40,72},{48,80},{56,88},{64,... | collective-permute-start | bytes 1474568 | tf_op jit(solution)/shard_map/ppermute | solution.py:41
  154.2 29.1 %collective-permute-start.16 = (bf16[4,80,768]{2,1,0:T(8,128)(2,1)}, bf16[4,80,768]{2,1,0:T(8,128)(2,1)}, u32[]{:S(2)}, u32[]{:S(2)}) collective-permute-start(bf16[4,80,768]{2,1,0:T(8,128)(2,1)} %slice.51), channel_id=1, source_target_pairs={{0,96},{8,104},{16,112},{24,120},{32,0},{40,8},{48,16},{56,24},{64... | collective-permute-start | bytes 1474568 | tf_op jit(solution)/shard_map/ppermute | solution.py:41
  157.4 25.8 %collective-permute-start.15 = (bf16[4,80,768]{2,1,0:T(8,128)(2,1)}, bf16[4,80,768]{2,1,0:T(8,128)(2,1)}, u32[]{:S(2)}, u32[]{:S(2)}) collective-permute-start(bf16[4,80,768]{2,1,0:T(8,128)(2,1)} %slice.50), channel_id=1, source_target_pairs={{0,32},{8,40},{16,48},{24,56},{32,64},{40,72},{48,80},{56,88},{64,... | collective-permute-start | bytes 1474568 | tf_op jit(solution)/shard_map/ppermute | solution.py:41
  205.8 15.0 %collective-permute-start.19 = (bf16[4,80,768]{2,1,0:T(8,128)(2,1)S(1)}, bf16[4,80,768]{2,1,0:T(8,128)(2,1)S(1)}, u32[]{:S(2)}, u32[]{:S(2)}) collective-permute-start(bf16[4,80,768]{2,1,0:T(8,128)(2,1)S(1)} %get-tuple-element.29), channel_id=1, source_target_pairs={{0,96},{8,104},{16,112},{24,120},{32,0},{40,8},{48,16},{56,24},{64... | collective-permute-start | bytes 1474568 | tf_op jit(solution)/shard_map/ppermute | solution.py:41
  209.1 15.7 %collective-permute-start.17 = (bf16[4,80,768]{2,1,0:T(8,128)(2,1)S(1)}, bf16[4,80,768]{2,1,0:T(8,128)(2,1)S(1)}, u32[]{:S(2)}, u32[]{:S(2)}) collective-permute-start(bf16[4,80,768]{2,1,0:T(8,128)(2,1)S(1)} %get-tuple-element.27), channel_id=1, source_target_pairs={{0,32},{8,40},{16,48},{24,56},{32,64},{40,72},{48,80},{56,88},{64,... | collective-permute-start | bytes 1474568 | tf_op jit(solution)/shard_map/ppermute | solution.py:41
  209.2 39.0 %collective-permute-start.22 = (bf16[4,80,768]{2,1,0:T(8,128)(2,1)S(1)}, bf16[4,80,768]{2,1,0:T(8,128)(2,1)S(1)}, u32[]{:S(2)}, u32[]{:S(2)}) collective-permute-start(bf16[4,80,768]{2,1,0:T(8,128)(2,1)S(1)} %get-tuple-element.32), channel_id=1, source_target_pairs={{0,32},{8,40},{16,48},{24,56},{32,64},{40,72},{48,80},{56,88},{64,... | collective-permute-start | bytes 1474568 | tf_op jit(solution)/shard_map/ppermute | solution.py:41
  209.2 35.5 %collective-permute-start.24 = (bf16[4,80,768]{2,1,0:T(8,128)(2,1)S(1)}, bf16[4,80,768]{2,1,0:T(8,128)(2,1)S(1)}, u32[]{:S(2)}, u32[]{:S(2)}) collective-permute-start(bf16[4,80,768]{2,1,0:T(8,128)(2,1)S(1)} %get-tuple-element.34), channel_id=1, source_target_pairs={{0,96},{8,104},{16,112},{24,120},{32,0},{40,8},{48,16},{56,24},{64... | collective-permute-start | bytes 1474568 | tf_op jit(solution)/shard_map/ppermute | solution.py:41
  221.0 31.4 %collective-permute-start.20 = (bf16[8,80,768]{2,1,0:T(8,128)(2,1)S(1)}, bf16[8,80,768]{2,1,0:T(8,128)(2,1)S(1)}, u32[]{:S(2)}, u32[]{:S(2)}) collective-permute-start(bf16[8,80,768]{2,1,0:T(8,128)(2,1)S(1)} %pad_maximum_fusion.1), channel_id=1, source_target_pairs={{0,96},{8,104},{16,112},{24,120},{32,0},{40,8},{48,16},{56,24},{64... | collective-permute-start | bytes 2949128 | tf_op jit(solution)/shard_map/ppermute | solution.py:41
  225.0 31.1 %collective-permute-start.18 = (bf16[8,80,768]{2,1,0:T(8,128)(2,1)S(1)}, bf16[8,80,768]{2,1,0:T(8,128)(2,1)S(1)}, u32[]{:S(2)}, u32[]{:S(2)}) collective-permute-start(bf16[8,80,768]{2,1,0:T(8,128)(2,1)S(1)} %pad_maximum_fusion), channel_id=1, source_target_pairs={{0,32},{8,40},{16,48},{24,56},{32,64},{40,72},{48,80},{56,88},{64,... | collective-permute-start | bytes 2949128 | tf_op jit(solution)/shard_map/ppermute | solution.py:41
  244.9 23.8 %collective-permute-start.25 = (bf16[8,80,768]{2,1,0:T(8,128)(2,1)S(1)}, bf16[8,80,768]{2,1,0:T(8,128)(2,1)S(1)}, u32[]{:S(2)}, u32[]{:S(2)}) collective-permute-start(bf16[8,80,768]{2,1,0:T(8,128)(2,1)S(1)} %pad_maximum_fusion.3), channel_id=1, source_target_pairs={{0,96},{8,104},{16,112},{24,120},{32,0},{40,8},{48,16},{56,24},{64... | collective-permute-start | bytes 2949128 | tf_op jit(solution)/shard_map/ppermute | solution.py:41
  248.4 23.8 %collective-permute-start.23 = (bf16[8,80,768]{2,1,0:T(8,128)(2,1)S(1)}, bf16[8,80,768]{2,1,0:T(8,128)(2,1)S(1)}, u32[]{:S(2)}, u32[]{:S(2)}) collective-permute-start(bf16[8,80,768]{2,1,0:T(8,128)(2,1)S(1)} %pad_maximum_fusion.2), channel_id=1, source_target_pairs={{0,32},{8,40},{16,48},{24,56},{32,64},{40,72},{48,80},{56,88},{64,... | collective-permute-start | bytes 2949128 | tf_op jit(solution)/shard_map/ppermute | solution.py:41
  256.4 15.8 %collective-permute-start.21 = (bf16[8,80,768]{2,1,0:T(8,128)(2,1)S(1)}, bf16[8,80,768]{2,1,0:T(8,128)(2,1)S(1)}, u32[]{:S(2)}, u32[]{:S(2)}) collective-permute-start(bf16[8,80,768]{2,1,0:T(8,128)(2,1)S(1)} %add_convert_fusion.1), channel_id=1, source_target_pairs={{0,16},{8,24},{16,0},{24,8},{32,48},{40,56},{48,32},{56,40},{64,80... | collective-permute-start | bytes 2949128 | tf_op jit(solution)/shard_map/ppermute | solution.py:41
  272.7 15.2 %copy-start.9 = (bf16[128,640]{1,0:T(8,128)(2,1)S(1)}, bf16[128,640]{1,0:T(8,128)(2,1)}, u32[]{:S(2)}) copy-start(bf16[128,640]{1,0:T(8,128)(2,1)} %copy-done.8) | copy-start | bytes 491524
  (11 other events, 42.6 us)

commit v2 on v1

--- a/solution.py
+++ b/solution.py
@@ -17,8 +17,6 @@
 SLICE = 768
 SHARDS = 16
 UNITS = 336
-MAIN = 256
-REST = UNITS - MAIN
 EPS = 1e-05
 F32 = jnp.float32
 BF16 = jnp.bfloat16
@@ -150,7 +148,8 @@
     )(starts, queries, paired, out_weight)
 
 
-def dispatch_kernel(terms_ref, residual_ref, gain_ref, placing_ref, hidden_ref, out_ref):
+def dispatch_kernel(terms_ref, residual_ref, gain_ref, placing_ref, *refs):
+    hidden_ref, out_ref = refs[-2:]
     hidden = residual_ref[...].astype(F32)
     for j in range(EXPERTS):
         hidden = hidden + terms_ref[j].astype(F32)
@@ -173,14 +172,16 @@
         ).astype(BF16)
 
 
-def dispatch(terms, residual, gain, placing):
+def dispatch(terms, residual, gain, placing, after):
+    whole = pl.BlockSpec(memory_space=pltpu.VMEM)
     return call(
         dispatch_kernel,
         (shape((TOK, SLICE), F32), shape((EXPERTS, CAP + AUX, SLICE))),
         24,
         2 * 10**8,
         5 * 10**6,
-    )(terms, residual, gain, placing)
+        in_specs=[whole] * 4 + [pl.BlockSpec(memory_space=pl.ANY)] * len(after),
+    )(terms, residual, gain, placing, *after)
 
 
 def norm_kernel(arrived_ref, out_ref):
@@ -215,124 +216,134 @@
 
 STEP = 2
 STEPS = EXPERTS // STEP
-
-
-def expert_kernel(parts, *refs):
-    count = len(parts)
-    xs, refs = refs[:count], refs[count:]
-    gate_own, gate_other, up_own, up_other, down_own, down_other = refs[:6]
-    outs = refs[6 : 6 + count]
-    rows_ref, gate_sum, up_sum, act_ref, gate_rest, up_rest, down_rest = refs[6 + count :]
-    step = pl.program_id(0)
-
-    @pl.when(step == 0)
-    def _():
-        gate_sum[...] = jnp.zeros_like(gate_sum)
-        up_sum[...] = jnp.zeros_like(up_sum)
-        gate_rest[...] = jnp.zeros_like(gate_rest)
-        up_rest[...] = jnp.zeros_like(up_rest)
-        down_rest[...] = jnp.zeros_like(down_rest)
-
-    @pl.when(step < STEPS)
-    def _():
-        for (shard, start, steps), x in zip(parts, xs):
-
-            @pl.when((step >= start) & (step < start + steps))
-            def _():
-                for k in range(STEP):
-                    rows_ref[shard * CAP : (shard + 1) * CAP, k * SLICE : (k + 1) * SLICE] = x[k]
-
-        rows = rows_ref[...]
-        for own, other, rest, total in (
-            (gate_own, gate_other, gate_rest, gate_sum),
-            (up_own, up_other, up_rest, up_sum),
-        ):
-            rest[:, :REST] = own[0, :, MAIN:]
-            rest[:, 128 : 128 + REST] = other[0, :, MAIN:]
-            total[:, :MAIN] += jnp.dot(rows, own[0, :, :MAIN], preferred_element_type=F32)
-            total[:, MAIN : 2 * MAIN] += jnp.dot(
-                rows, other[0, :, :MAIN], preferred_element_type=F32
-            )
-            total[:, 2 * MAIN :] += jnp.dot(rows, rest[...], preferred_element_type=F32)
-
-    @pl.when(step == STEPS)
-    def _():
-        gate = gate_sum[...]
-        act_ref[...] = (gate / (1.0 + jnp.exp(-gate)) * up_sum[...]).astype(BF16)
-
-    @pl.when(step >= STEPS)
-    def _():
-        down_rest[:REST] = down_own[0, MAIN:]
-        down_rest[128 : 128 + REST] = down_other[0, MAIN:]
-        for k in range(STEP):
-            cols = slice(k * SLICE, (k + 1) * SLICE)
-            result = jnp.dot(act_ref[:, :MAIN], down_own[0, :MAIN, cols], preferred_element_type=F32)
-            result += jnp.dot(
-                act_ref[:, MAIN : 2 * MAIN], down_other[0, :MAIN, cols], preferred_element_type=F32
-            )
-            result += jnp.dot(
-                act_ref[:, 2 * MAIN :], down_rest[:, cols], preferred_element_type=F32
-            )
-            result = result.astype(BF16)
-            for (shard, start, steps), out in zip(parts, outs):
-
-                @pl.when((step >= STEPS + start) & (step < STEPS + start + steps))
-                def _():
-                    out[k] = result[shard * CAP : (shard + 1) * CAP]
-
-
-def expert(shards, weights):
-    parts, arrays = [], []
-    for number, split in enumerate(shards):
-        start = 0
-        for array in split:
-            steps = array.shape[0] // STEP
-            parts.append((number, start, steps))
-            arrays.append(array)
-            start += steps
-    total = CAP * len(shards)
-    width = STEP * SLICE
-
-    def rows_spec(part, late):
-        _, start, steps = part
-        return pl.BlockSpec(
-            (STEP, CAP, SLICE),
-            lambda i: (jnp.clip(i - start - late, 0, steps - 1), 0, 0),
-        )
-
-    across = pl.BlockSpec((1, width, UNITS), lambda i: (0, jnp.minimum(i, STEPS - 1), 0))
-    along = pl.BlockSpec((1, UNITS, width), lambda i: (0, 0, jnp.maximum(i - STEPS, 0)))
-    outs = call(
-        functools.partial(expert_kernel, parts),
-        tuple(shape(array.shape) for array in arrays),
+WIDTH = STEP * SLICE
+HELD = 2 * UNITS
+
+
+def expert_kernel(pieces_in, pieces_out, n_in, *refs):
+    xs, refs = refs[:n_in], refs[n_in:]
+    weights, outs = refs[:6], refs[6:-8]
+    rows_ref, gate_ref, up_ref, down_ref, gate_sum, up_sum, act_ref, ready = refs[-8:]
+
+    def copies(step):
+        found = []
+        for number, (held, late) in enumerate(((gate_ref, 0), (up_ref, 0), (down_ref, STEPS))):
+            if not 0 <= step - late < STEPS:
+                continue
+            columns = pl.ds((step - late) * WIDTH, WIDTH)
+            for core in range(2):
+                found.append(
+                    pltpu.make_async_copy(
+                        weights[2 * number + core].at[:, columns],
+                        held.at[pl.ds(core * UNITS, UNITS), columns],
+                        ready.at[number * 2 + core, step - late],
+                    )
+                )
+        return found
+
+    def start(step):
+        for copy in copies(step):
+            copy.start()
+
+    start(0)
+    start(1)
+    for step in range(2 * STEPS):
+        if step < STEPS:
+            for shard, split in enumerate(pieces_in):
+                block = 0
+                for number, first, count in split:
+                    for k in range(first, first + count):
+                        if block // STEP == step:
+                            rows_ref[
+                                shard * CAP : (shard + 1) * CAP, block * SLICE : (block + 1) * SLICE
+                            ] = xs[number][k]
+                        block += 1
+        for copy in copies(step):
+            copy.wait()
+        if step + 2 < 2 * STEPS:
+            start(step + 2)
+        if step < STEPS:
+            columns = slice(step * WIDTH, (step + 1) * WIDTH)
+            rows = rows_ref[:, columns]
+            for held, total in ((gate_ref, gate_sum), (up_ref, up_sum)):
+                term = lax.dot_general(
+                    rows, held[:, columns], (((1,), (1,)), ((), ())), preferred_element_type=F32
+                )
+                if step == 0:
+                    total[...] = term
+                else:
+                    total[...] += term
+        if step == STEPS - 1:
+            gate = gate_sum[...]
+            act_ref[...] = (gate / (1.0 + jnp.exp(-gate)) * up_sum[...]).astype(BF16)
+        if step >= STEPS:
+            for now in range((step - STEPS) * STEP, (step - STEPS + 1) * STEP):
+                result = jnp.dot(
+                    act_ref[...],
+                    down_ref[:, now * SLICE : (now + 1) * SLICE],
+                    preferred_element_type=F32,
+                ).astype(BF16)
+                for shard, split in enumerate(pieces_out):
+                    block = 0
+                    for number, first, count in split:
+                        if block <= now < block + count:
+                            outs[number][first + now - block] = result[
+                                shard * CAP : (shard + 1) * CAP
+                            ]
+                        block += count
+
+
+def expert(arrays, pieces_in, sizes, pieces_out, weights):
+    total = CAP * len(pieces_in)
+    whole = pl.BlockSpec(memory_space=pltpu.VMEM)
+    apart = pl.BlockSpec(memory_space=pl.ANY)
+    return call(
+        functools.partial(expert_kernel, pieces_in, pieces_out, len(arrays)),
+        tuple(shape((size, CAP, SLICE)) for size in sizes),
         44,
         total * D * 2 * UNITS * 6,
-        27 * 10**6,
-        grid=(2 * STEPS,),
-        in_specs=[rows_spec(part, 0) for part in parts] + [across] * 4 + [along] * 2,
-        out_specs=tuple(rows_spec(part, STEPS) for part in parts),
+        25 * 10**6,
+        in_specs=[whole] * len(arrays) + [apart] * 6,
+        out_specs=(whole,) * len(sizes),
         scratch_shapes=[
-            pltpu.VMEM((total, width), BF16),
-            pltpu.VMEM((total, 3 * MAIN), F32),
-            pltpu.VMEM((total, 3 * MAIN), F32),
-            pltpu.VMEM((total, 3 * MAIN), BF16),
-            pltpu.VMEM((width, MAIN), BF16),
-            pltpu.VMEM((width, MAIN), BF16),
-            pltpu.VMEM((MAIN, width), BF16),
+            pltpu.VMEM((total, D), BF16),
+            pltpu.VMEM((HELD, D), BF16),
+            pltpu.VMEM((HELD, D), BF16),
+            pltpu.VMEM((HELD, D), BF16),
+            pltpu.VMEM((total, HELD), F32),
+            pltpu.VMEM((total, HELD), F32),
+            pltpu.VMEM((total, HELD), BF16),
+            pltpu.SemaphoreType.DMA((6, STEPS)),
         ],
     )(*arrays, *weights)
-    results, taken = [], 0
-    for split in shards:
-        results.append(list(outs[taken : taken + len(split)]))
-        taken += len(split)
-    return results
-
-
-def add(*values):
-    total = values[0].astype(F32)
-    for value in values[1:]:
-        total = total + value.astype(F32)
-    return total.astype(BF16)
+
+
+def join_kernel(plans, *refs):
+    ins, outs = refs, refs[len(refs) - len(plans) :]
+    for (size, terms), out in zip(plans, outs):
+        for block in range(size):
+            total = None
+            for number, first, into, count in terms:
+                if into <= block < into + count:
+                    value = ins[number][first + block - into]
+                    if total is None:
+                        total = value
+                    else:
+                        total = total.astype(F32) + value.astype(F32)
+            out[block] = total.astype(BF16)
+
+
+def join(plans, *arrays, after=()):
+    whole = pl.BlockSpec(memory_space=pltpu.VMEM)
+    return call(
+        functools.partial(join_kernel, plans),
+        tuple(shape((size, CAP, SLICE)) for size, _ in plans),
+        16,
+        10**7,
+        8 * 10**6,
+        in_specs=[whole] * len(arrays) + [pl.BlockSpec(memory_space=pl.ANY)] * len(after),
+        out_specs=(whole,) * len(plans),
+    )(*arrays, *after)
 
 
 def combine_kernel(hidden_ref, high_ref, low_ref, outputs_ref, mixed_ref):
@@ -374,38 +385,108 @@
         for dz in (0, 1)
     ]
     starts = jnp.stack(starts + [ctx * TOK]).astype(jnp.int32)
-    placing, high, low = routing(expert_ids, gate_scores)
+    placing, share_high, share_low = routing(expert_ids, gate_scores)
     weights = []
-    for weight in (gate_weight, up_weight, down_weight):
+    for weight in (gate_weight[0].T, up_weight[0].T, down_weight[0]):
         weights += [weight, send(weight, dc=1)]
 
     term = attention(starts, queries, paired, out_weight)
     terms = lax.all_to_all(term, "exp", 0, 0, tiled=True)
-    hidden, outgoing = dispatch(terms, residual, ln_gain[None], placing)
+    hidden, outgoing = dispatch(terms, residual, ln_gain[None], placing, weights[1::2])
     arrived = lax.all_to_all(outgoing, "exp", 0, 0, tiled=True)
     mine = norm(arrived)
 
-    half = EXPERTS // 2
     back, ahead, across = send(mine, dy=1), send(mine, dy=-1), send(mine, dz=1)
-    across_back, across_ahead = send(across, dy=1), send(across, dy=-1)
-    far = [send(back[:half], dy=1), send(ahead[half:], dy=-1)]
-    across_far = [send(across_back[:half], dy=1), send(across_ahead[half:], dy=-1)]
-    first = expert([[mine], [across], [back], [ahead]], weights)
-    second = expert([[across_back], [across_ahead], far, across_far], weights)
-    part = [first[0][0], first[2][0], first[3][0], second[2]]
-    across_part = [first[1][0], second[0][0], second[1][0], second[3]]
-
-    def ring(part):
-        mine, back, ahead, far = part
-        low_half, high_half = send(far[0], dy=1), send(far[1], dy=-1)
-        ahead = jnp.concatenate([add(ahead[:half], low_half), ahead[half:]])
-        back = jnp.concatenate([back[:half], add(back[half:], high_half)])
-        return mine, send(ahead, dy=1), send(back, dy=-1)
-
-    across_sum = send(add(*ring(across_part)), dz=1)
-    result = add(across_sum, *ring(part))
+    low, high, across_a, both_b = join(
+        (
+            (4, ((0, 0, 0, 4),)),
+            (4, ((1, 4, 0, 4),)),
+            (5, ((2, 0, 0, 5),)),
+            (6, ((0, 5, 0, 3), (1, 5, 3, 3))),
+        ),
+        back,
+        ahead,
+        across,
+    )
+    far_low, far_high = send(low, dy=1), send(high, dy=-1)
+    across_back, across_ahead = send(across_a, dy=1), send(across_a, dy=-1)
+    across_b = send(both_b, dz=1)
+    mine, across, back, ahead = expert(
+        [mine, across, back, ahead],
+        [[(k, 0, 8)] for k in range(4)],
+        (8,) * 4,
+        [[(k, 0, 8)] for k in range(4)],
+        weights,
+    )
+    low, high, far_b = join(
+        (
+            (3, ((0, 0, 0, 3),)),
+            (2, ((1, 3, 0, 2),)),
+            (3, ((3, 1, 0, 3),)),
+        ),
+        across_back,
+        across_ahead,
+        far_low,
+        far_high,
+        across_b,
+        after=(mine,),
+    )
+    across_far = [send(low, dy=1), send(high, dy=-1), send(far_b, dz=1)]
+    far, across_back, across_ahead, across_b, far_low, far_high, far_b = expert(
+        [far_low, far_high, across_back, across_ahead, across_b] + across_far,
+        [
+            [(0, 0, 4), (1, 0, 4)],
+            [(2, 0, 5), (4, 0, 3)],
+            [(3, 0, 5), (4, 3, 3)],
+            [(5, 0, 3), (6, 0, 2), (7, 0, 3)],
+        ],
+        (8, 5, 5, 6, 3, 2, 3),
+        [
+            [(0, 0, 8)],
+            [(1, 0, 5), (3, 0, 3)],
+            [(2, 0, 5), (3, 3, 3)],
+            [(4, 0, 3), (5, 0, 2), (6, 0, 3)],
+        ],
+        weights,
+    )
+    across_ahead, across_back, low, high = join(
+        (
+            (5, ((0, 0, 0, 5), (3, 0, 0, 3))),
+            (5, ((1, 0, 0, 5), (4, 0, 3, 2))),
+            (4, ((2, 0, 0, 4),)),
+            (4, ((2, 4, 0, 4), (5, 0, 1, 3))),
+        ),
+        across_ahead,
+        across_back,
+        far,
+        send(far_low, dy=1),
+        send(far_high, dy=-1),
+        send(far_b, dz=1),
+    )
+    across, ahead, back = join(
+        (
+            (8, ((0, 0, 0, 8), (3, 0, 0, 5), (4, 0, 0, 5))),
+            (8, ((1, 0, 0, 8), (5, 0, 0, 4), (7, 3, 5, 3))),
+            (8, ((2, 0, 0, 8), (6, 0, 4, 4), (7, 0, 5, 3))),
+        ),
+        across,
+        ahead,
+        back,
+        send(across_ahead, dy=1),
+        send(across_back, dy=-1),
+        send(low, dy=1),
+        send(high, dy=-1),
+        send(across_b, dz=1),
+    )
+    (result,) = join(
+        ((8, tuple((number, 0, 0, 8) for number in range(4))),),
+        mine,
+        send(ahead, dy=1),
+        send(back, dy=-1),
+        send(across, dz=1),
+    )
     outputs = lax.all_to_all(result, "exp", 0, 0, tiled=True)
-    return combine(hidden, high, low, outputs)
+    return combine(hidden, share_high, share_low, outputs)
 
 
 def solution(mesh):

time: 290 us -> 251 us (0.87)
  local copies, waits for them, and re-layouts: 35.5 us -> 1.51 us
  waiting for transfers between devices: 128 us -> 102 us
  blocking collectives: 15.2 us -> 33.3 us
  starting transfers between devices: 51 us -> 65.2 us
  Pallas kernels: 55.7 us -> 43.4 us
    all_to_all x0 -> x1, blocking collectives: none -> 19.7 us  [body(): arrived = lax.all_to_all(outgoing, 'exp', 0, 0, tiled=True)]
    ppermute x26 -> x30, starting transfers between devices: 42 us -> 60.3 us  [send(): return lax.ppermute(block, 'ctx', route(dy, dz, dc))]
    unnamed x37 -> x15, local copies, waits for them, and re-layouts: 19 us -> 1.29 us
    all_to_all x1 -> x0, waiting for transfers between devices: 17 us -> none  [body(): arrived = lax.all_to_all(outgoing, 'exp', 0, 0, tiled=True)]
    ppermute x2 -> x0, local copies, waits for them, and re-layouts: 12.9 us -> none  [send(): return lax.ppermute(block, 'ctx', route(dy, dz, dc))]
    pallas_call x2 -> x7, Pallas kernels: 39.4 us -> 28.2 us  [the longest x2 26.6 us: expert(): call(functools.partial(expert_kernel, pieces_in, pieces_out, len(arrays))...]
    ppermute x26 -> x30, waiting for transfers between devices: 92.6 us -> 81.6 us  [send(): return lax.ppermute(block, 'ctx', route(dy, dz, dc))]
    all_to_all x1 -> x0, starting transfers between devices: 3.79 us -> none  [body(): arrived = lax.all_to_all(outgoing, 'exp', 0, 0, tiled=True)]
  transfers between devices with their start and end apart: 28 -> 31, of which waited for: 16 -> 17; matrix products, arithmetic and copies ran while one was open for 11% -> 1% of each run, Pallas kernels for 8% -> 10%
where the time goes in v2:
time: 251 us; the launch traced here: 247 us
  waiting for transfers between devices  102 us (41%)
  starting transfers between devices  65.2 us (26%)
  Pallas kernels  43.4 us (17%)
  blocking collectives  33.3 us (13%)
    ppermute x30, waiting for transfers between devices, send(): return lax.ppermute(block, 'ctx', route(dy, dz, dc))  81.6 us
    ppermute x30, starting transfers between devices, send(): return lax.ppermute(block, 'ctx', route(dy, dz, dc))  60.3 us
    pallas_call x2, Pallas kernels, expert(): call(functools.partial(expert_kernel, pieces_in, pieces_out, len(arrays))...  26.6 us
    all_to_all x1, waiting for transfers between devices, body(): terms = lax.all_to_all(term, 'exp', 0, 0, tiled=True)  20.1 us
    all_to_all x1, blocking collectives, body(): arrived = lax.all_to_all(outgoing, 'exp', 0, 0, tiled=True)  19.7 us
    all_to_all x1, blocking collectives, body(): outputs = lax.all_to_all(result, 'exp', 0, 0, tiled=True)  13.6 us
    pallas_call x1, Pallas kernels, attention(): call(attention_kernel, shape((EXPERTS, TOK, SLICE)), 48, 2 * 10 ** 9, 13...  9.95 us
  transfers between devices with their start and end apart: 31, of which 17 were waited for; matrix products, arithmetic and copies ran while one was open for 1% of the time, Pallas kernels for 10%

profile of v2, /device:TPU:0, one launch (start us, length us, event | category | flops | bytes accessed | tf_op | source)
XLA Modules:
  0.0 247.3 jit_solution(7456820002034558370)
XLA Ops:
  1.3 4.0 %collective-permute-start = (bf16[1,2,128,128]{3,2,1,0:T(8,128)(2,1)S(1)}, bf16[1,2,128,128]{3,2,1,0:T(8,128)(2,1)S(1)}, u32[]{:S(2)}, u32[]{:S(2)}) collective-permute-start(bf16[1,2,128,128]{3,2,1,0:T(8,128)(2,1)S(1)} %maximum_bitcast_fusion), channel_id=1, source_target_pairs={{0,16},{8,24},{16,0},{24,8},{32,48},{40,56},{48,32},{56,40},{64,80... | collective-permute-start | bytes 196616 | tf_op jit(solution)/shard_map/ppermute | solution.py:39
  5.3 2.8 %collective-permute-done = bf16[1,2,128,128]{3,2,1,0:T(8,128)(2,1)S(1)} collective-permute-done((bf16[1,2,128,128]{3,2,1,0:T(8,128)(2,1)S(1)}, bf16[1,2,128,128]{3,2,1,0:T(8,128)(2,1)S(1)}, u32[]{:S(2)}, u32[]{:S(2)}) %collective-permute-start) | collective-permute-done | bytes 65568 | tf_op jit(solution)/shard_map/ppermute | solution.py:39
  12.3 2.5 %collective-permute-done.1 = bf16[2,2,128,128]{3,2,1,0:T(8,128)(2,1)S(1)} collective-permute-done((bf16[2,2,128,128]{3,2,1,0:T(8,128)(2,1)S(1)}, bf16[2,2,128,128]{3,2,1,0:T(8,128)(2,1)S(1)}, u32[]{:S(2)}, u32[]{:S(2)}) %collective-permute-start.1) | collective-permute-done | bytes 131104 | tf_op jit(solution)/shard_map/ppermute | solution.py:39
  16.8 4.4 %collective-permute-done.3 = bf16[2,2,128,128]{3,2,1,0:T(8,128)(2,1)S(1)} collective-permute-done((bf16[2,2,128,128]{3,2,1,0:T(8,128)(2,1)S(1)}, bf16[2,2,128,128]{3,2,1,0:T(8,128)(2,1)S(1)}, u32[]{:S(2)}, u32[]{:S(2)}) %collective-permute-start.3) | collective-permute-done | bytes 131104 | tf_op jit(solution)/shard_map/ppermute | solution.py:39
  24.3 10.0 %shard_map.109 = bf16[8,128,768]{2,1,0:T(8,128)(2,1)} custom-call(s32[17]{0:T(128)S(1)} %stack.80.starts_ref, bf16[128,768]{1,0:T(8,128)(2,1)S(1)} %copy-done.1, bf16[16,2,128,128]{3,2,1,0:T(8,128)(2,1)S(1)} %constant_dynamic-update-slice_fusion.5.paired_ref, bf16[768,6144]{1,0:T(8,128)(2,1)} %weight_ref.1), custom_call_target="tpu_custom_call" | custom-call | flops 2000000000 | bytes 13000000 | tf_op jit(solution)/shard_map/pallas_call | solution.py:134
  34.3 4.8 %all-to-all-start = ((bf16[8,128,768]{2,1,0:T(8,128)(2,1)}), bf16[8,128,768]{2,1,0:T(8,128)(2,1)S(1)}, u32[]{:S(2)}, u32[]{:S(2)}) async-start(bf16[8,128,768]{2,1,0:T(8,128)(2,1)} %shard_map.109), calls=%async_computation | async-start | bytes 3145728 | tf_op jit(solution)/shard_map/all_to_all | solution.py:394
  40.6 20.1 %all-to-all-done.terms_ref = bf16[8,128,768]{2,1,0:T(8,128)(2,1)S(1)} async-done(((bf16[8,128,768]{2,1,0:T(8,128)(2,1)}), bf16[8,128,768]{2,1,0:T(8,128)(2,1)S(1)}, u32[]{:S(2)}, u32[]{:S(2)}) %all-to-all-start) | async-done | bytes 1572896 | tf_op jit(solution)/shard_map/all_to_all | solution.py:394
  61.6 19.7 %all_to_all.15.arrived_ref = bf16[8,96,768]{2,1,0:T(8,128)(2,1)S(1)} all-to-all(bf16[8,96,768]{2,1,0:T(8,128)(2,1)S(1)} %get-tuple-element.39), channel_id=1, replica_groups=mesh['ctx'=16,'exp'=8] {'exp'}, dimensions={0} | all-to-all | bytes 2359296 | tf_op jit(solution)/shard_map/all_to_all | solution.py:396
  81.3 2.0 shard_map.112.refs_0_
  85.4 3.9 %collective-permute-start.8 = (bf16[8,80,768]{2,1,0:T(8,128)(2,1)S(1)}, bf16[8,80,768]{2,1,0:T(8,128)(2,1)S(1)}, u32[]{:S(2)}, u32[]{:S(2)}) collective-permute-start(bf16[8,80,768]{2,1,0:T(8,128)(2,1)S(1)} %shard_map.112.refs_0_), channel_id=1, source_target_pairs={{0,16},{8,24},{16,0},{24,8},{32,48},{40,56},{48,32},{56,40},{64,80... | collective-permute-start | bytes 2949128 | tf_op jit(solution)/shard_map/ppermute | solution.py:39
  89.3 15.7 %collective-permute-done.10.refs_3_.refs_1_ = bf16[8,80,768]{2,1,0:T(8,128)(2,1)S(1)} collective-permute-done((bf16[8,80,768]{2,1,0:T(8,128)(2,1)S(1)}, bf16[8,80,768]{2,1,0:T(8,128)(2,1)S(1)}, u32[]{:S(2)}, u32[]{:S(2)}) %collective-permute-start.10) | collective-permute-done | bytes 983072 | tf_op jit(solution)/shard_map/ppermute | solution.py:39
  105.0 2.7 %collective-permute-done.9.refs_2_.refs_0_ = bf16[8,80,768]{2,1,0:T(8,128)(2,1)S(1)} collective-permute-done((bf16[8,80,768]{2,1,0:T(8,128)(2,1)S(1)}, bf16[8,80,768]{2,1,0:T(8,128)(2,1)S(1)}, u32[]{:S(2)}, u32[]{:S(2)}) %collective-permute-start.9) | collective-permute-done | bytes 983072 | tf_op jit(solution)/shard_map/ppermute | solution.py:39
  108.8 3.0 %collective-permute-start.14 = (bf16[5,80,768]{2,1,0:T(8,128)(2,1)S(1)}, bf16[5,80,768]{2,1,0:T(8,128)(2,1)S(1)}, u32[]{:S(2)}, u32[]{:S(2)}) collective-permute-start(bf16[5,80,768]{2,1,0:T(8,128)(2,1)S(1)} %get-tuple-element.46), channel_id=1, source_target_pairs={{0,96},{8,104},{16,112},{24,120},{32,0},{40,8},{48,16},{56,24},{64... | collective-permute-start | bytes 1843208 | tf_op jit(solution)/shard_map/ppermute | solution.py:39
  111.8 3.3 %collective-permute-start.12 = (bf16[4,80,768]{2,1,0:T(8,128)(2,1)S(1)}, bf16[4,80,768]{2,1,0:T(8,128)(2,1)S(1)}, u32[]{:S(2)}, u32[]{:S(2)}) collective-permute-start(bf16[4,80,768]{2,1,0:T(8,128)(2,1)S(1)} %get-tuple-element.45), channel_id=1, source_target_pairs={{0,96},{8,104},{16,112},{24,120},{32,0},{40,8},{48,16},{56,24},{64... | collective-permute-start | bytes 1474568 | tf_op jit(solution)/shard_map/ppermute | solution.py:39
  115.1 3.2 %collective-permute-start.15 = (bf16[6,80,768]{2,1,0:T(8,128)(2,1)S(1)}, bf16[6,80,768]{2,1,0:T(8,128)(2,1)S(1)}, u32[]{:S(2)}, u32[]{:S(2)}) collective-permute-start(bf16[6,80,768]{2,1,0:T(8,128)(2,1)S(1)} %get-tuple-element.47), channel_id=1, source_target_pairs={{0,16},{8,24},{16,0},{24,8},{32,48},{40,56},{48,32},{56,40},{64,80... | collective-permute-start | bytes 2211848 | tf_op jit(solution)/shard_map/ppermute | solution.py:39
  118.3 13.3 %shard_map.113 = (bf16[8,80,768]{2,1,0:T(8,128)(2,1)S(1)}, bf16[8,80,768]{2,1,0:T(8,128)(2,1)S(1)}, bf16[8,80,768]{2,1,0:T(8,128)(2,1)S(1)}, bf16[8,80,768]{2,1,0:T(8,128)(2,1)S(1)}) custom-call(bf16[8,80,768]{2,1,0:T(8,128)(2,1)S(1)} %shard_map.112.refs_0_, bf16[8,80,768]{2,1,0:T(8,128)(2,1)S(1)} %collective-permute-done.8.refs_1_.refs_2_, ...), custom_call_target="tpu_custom_call" | custom-call | flops 7927234560 | bytes 25000000 | tf_op jit(solution)/shard_map/pallas_call | solution.py:300
  131.7 4.6 %collective-permute-done.11.refs_2_.refs_0_ = bf16[4,80,768]{2,1,0:T(8,128)(2,1)S(1)} collective-permute-done((bf16[4,80,768]{2,1,0:T(8,128)(2,1)S(1)}, bf16[4,80,768]{2,1,0:T(8,128)(2,1)S(1)}, u32[]{:S(2)}, u32[]{:S(2)}) %collective-permute-start.11) | collective-permute-done | bytes 491552 | tf_op jit(solution)/shard_map/ppermute | solution.py:39
  136.4 3.3 %collective-permute-start.18 = (bf16[3,80,768]{2,1,0:T(8,128)(2,1)S(1)}, bf16[3,80,768]{2,1,0:T(8,128)(2,1)S(1)}, u32[]{:S(2)}, u32[]{:S(2)}) collective-permute-start(bf16[3,80,768]{2,1,0:T(8,128)(2,1)S(1)} %get-tuple-element.50), channel_id=1, source_target_pairs={{0,16},{8,24},{16,0},{24,8},{32,48},{40,56},{48,32},{56,40},{64,80... | collective-permute-start | bytes 1105928 | tf_op jit(solution)/shard_map/ppermute | solution.py:39
  139.7 12.7 %collective-permute-start.17 = (bf16[2,80,768]{2,1,0:T(8,128)(2,1)S(1)}, bf16[2,80,768]{2,1,0:T(8,128)(2,1)S(1)}, u32[]{:S(2)}, u32[]{:S(2)}) collective-permute-start(bf16[2,80,768]{2,1,0:T(8,128)(2,1)S(1)} %get-tuple-element.49), channel_id=1, source_target_pairs={{0,96},{8,104},{16,112},{24,120},{32,0},{40,8},{48,16},{56,24},{64... | collective-permute-start | bytes 737288 | tf_op jit(solution)/shard_map/ppermute | solution.py:39
  152.4 3.7 %collective-permute-done.17.refs_6_ = bf16[2,80,768]{2,1,0:T(8,128)(2,1)S(1)} collective-permute-done((bf16[2,80,768]{2,1,0:T(8,128)(2,1)S(1)}, bf16[2,80,768]{2,1,0:T(8,128)(2,1)S(1)}, u32[]{:S(2)}, u32[]{:S(2)}) %collective-permute-start.17) | collective-permute-done | bytes 245792 | tf_op jit(solution)/shard_map/ppermute | solution.py:39
  156.1 13.3 %shard_map.116 = (bf16[8,80,768]{2,1,0:T(8,128)(2,1)S(1)}, bf16[5,80,768]{2,1,0:T(8,128)(2,1)S(1)}, bf16[5,80,768]{2,1,0:T(8,128)(2,1)S(1)}, bf16[6,80,768]{2,1,...) custom-call(bf16[4,80,768]{2,1,0:T(8,128)(2,1)S(1)} %collective-perm, ...), custom_call_target="tpu_custom_call" | custom-call | flops 7927234560 | bytes 25000000 | tf_op jit(solution)/shard_map/pallas_call | solution.py:300
  169.9 3.7 %collective-permute-start.20 = (bf16[2,80,768]{2,1,0:T(8,128)(2,1)S(1)}, bf16[2,80,768]{2,1,0:T(8,128)(2,1)S(1)}, u32[]{:S(2)}, u32[]{:S(2)}) collective-permute-start(bf16[2,80,768]{2,1,0:T(8,128)(2,1)S(1)} %get-tuple-element.55), channel_id=1, source_target_pairs={{0,96},{8,104},{16,112},{24,120},{32,0},{40,8},{48,16},{56,24},{64... | collective-permute-start | bytes 737288 | tf_op jit(solution)/shard_map/ppermute | solution.py:39
  173.6 3.2 %collective-permute-start.26 = (bf16[6,80,768]{2,1,0:T(8,128)(2,1)S(1)}, bf16[6,80,768]{2,1,0:T(8,128)(2,1)S(1)}, u32[]{:S(2)}, u32[]{:S(2)}) collective-permute-start(bf16[6,80,768]{2,1,0:T(8,128)(2,1)S(1)} %get-tuple-element.61), channel_id=1, source_target_pairs={{0,16},{8,24},{16,0},{24,8},{32,48},{40,56},{48,32},{56,40},{64,80... | collective-permute-start | bytes 2211848 | tf_op jit(solution)/shard_map/ppermute | solution.py:39
  176.8 3.1 %collective-permute-done.20.refs_4_ = bf16[2,80,768]{2,1,0:T(8,128)(2,1)S(1)} collective-permute-done((bf16[2,80,768]{2,1,0:T(8,128)(2,1)S(1)}, bf16[2,80,768]{2,1,0:T(8,128)(2,1)S(1)}, u32[]{:S(2)}, u32[]{:S(2)}) %collective-permute-start.20) | collective-permute-done | bytes 245792 | tf_op jit(solution)/shard_map/ppermute | solution.py:39
  179.9 2.3 collective-permute-done.19.refs_3_
  184.5 2.0 collective-permute-start.23
  187.5 2.3 collective-permute-start.25
  190.5 16.5 %collective-permute-done.24.refs_5_ = bf16[4,80,768]{2,1,0:T(8,128)(2,1)S(1)} collective-permute-done((bf16[4,80,768]{2,1,0:T(8,128)(2,1)S(1)}, bf16[4,80,768]{2,1,0:T(8,128)(2,1)S(1)}, u32[]{:S(2)}, u32[]{:S(2)}) %collective-permute-start.24) | collective-permute-done | bytes 491552 | tf_op jit(solution)/shard_map/ppermute | solution.py:39
  208.6 2.5 %collective-permute-start.28 = (bf16[8,80,768]{2,1,0:T(8,128)(2,1)S(1)}, bf16[8,80,768]{2,1,0:T(8,128)(2,1)S(1)}, u32[]{:S(2)}, u32[]{:S(2)}) collective-permute-start(bf16[8,80,768]{2,1,0:T(8,128)(2,1)S(1)} %get-tuple-element.63), channel_id=1, source_target_pairs={{0,96},{8,104},{16,112},{24,120},{32,0},{40,8},{48,16},{56,24},{64... | collective-permute-start | bytes 2949128 | tf_op jit(solution)/shard_map/ppermute | solution.py:39
  212.4 11.1 %collective-permute-done.27.refs_1_ = bf16[8,80,768]{2,1,0:T(8,128)(2,1)S(1)} collective-permute-done((bf16[8,80,768]{2,1,0:T(8,128)(2,1)S(1)}, bf16[8,80,768]{2,1,0:T(8,128)(2,1)S(1)}, u32[]{:S(2)}, u32[]{:S(2)}) %collective-permute-start.27) | collective-permute-done | bytes 983072 | tf_op jit(solution)/shard_map/ppermute | solution.py:39
  223.4 8.5 %collective-permute-done.29.refs_3_ = bf16[8,80,768]{2,1,0:T(8,128)(2,1)S(1)} collective-permute-done((bf16[8,80,768]{2,1,0:T(8,128)(2,1)S(1)}, bf16[8,80,768]{2,1,0:T(8,128)(2,1)S(1)}, u32[]{:S(2)}, u32[]{:S(2)}) %collective-permute-start.29) | collective-permute-done | bytes 983072 | tf_op jit(solution)/shard_map/ppermute | solution.py:39
  232.4 13.6 %all_to_all.16.outputs_ref = bf16[8,80,768]{2,1,0:T(8,128)(2,1)S(1)} all-to-all(bf16[8,80,768]{2,1,0:T(8,128)(2,1)S(1)} %shard_map.119), channel_id=1, replica_groups=mesh['ctx'=16,'exp'=8] {'exp'}, dimensions={0} | all-to-all | bytes 1966080 | tf_op jit(solution)/shard_map/all_to_all | solution.py:488
  (66 shorter events, 25.0 us)
Async XLA Ops:
  0.0 60.7 %collective-permute-start.5 = (bf16[336,6144]{1,0:T(8,128)(2,1)}, bf16[336,6144]{1,0:T(8,128)(2,1)}, u32[]{:S(2)}, u32[]{:S(2)}) collective-permute-start(bf16[336,6144]{1,0:T(8,128)(2,1)} %bitcast.36), channel_id=1, source_target_pairs={{0,8},{8,0},{16,24},{24,16},{32,40},{40,32},{48,56},{56,48},{64,72... | collective-permute-start | bytes 12386312 | tf_op jit(solution)/shard_map/ppermute | solution.py:39
  0.0 60.7 %collective-permute-start.6 = (bf16[336,6144]{1,0:T(8,128)(2,1)}, bf16[336,6144]{1,0:T(8,128)(2,1)}, u32[]{:S(2)}, u32[]{:S(2)}) collective-permute-start(bf16[336,6144]{1,0:T(8,128)(2,1)} %bitcast.39), channel_id=1, source_target_pairs={{0,8},{8,0},{16,24},{24,16},{32,40},{40,32},{48,56},{56,48},{64,72... | collective-permute-start | bytes 12386312 | tf_op jit(solution)/shard_map/ppermute | solution.py:39
  0.5 60.2 %collective-permute-start.7 = (bf16[336,6144]{1,0:T(8,128)(2,1)}, bf16[336,6144]{1,0:T(8,128)(2,1)}, u32[]{:S(2)}, u32[]{:S(2)}) collective-permute-start(bf16[336,6144]{1,0:T(8,128)(2,1)} %bitcast.42), channel_id=1, source_target_pairs={{0,8},{8,0},{16,24},{24,16},{32,40},{40,32},{48,56},{56,48},{64,72... | collective-permute-start | bytes 12386312 | tf_op jit(solution)/shard_map/ppermute | solution.py:39
  1.3 6.8 %collective-permute-start = (bf16[1,2,128,128]{3,2,1,0:T(8,128)(2,1)S(1)}, bf16[1,2,128,128]{3,2,1,0:T(8,128)(2,1)S(1)}, u32[]{:S(2)}, u32[]{:S(2)}) collective-permute-start(bf16[1,2,128,128]{3,2,1,0:T(8,128)(2,1)S(1)} %maximum_bitcast_fusion), channel_id=1, source_target_pairs={{0,16},{8,24},{16,0},{24,8},{32,48},{40,56},{48,32},{56,40},{64,80... | collective-permute-start | bytes 196616 | tf_op jit(solution)/shard_map/ppermute | solution.py:39
  8.1 6.7 %collective-permute-start.1 = (bf16[2,2,128,128]{3,2,1,0:T(8,128)(2,1)S(1)}, bf16[2,2,128,128]{3,2,1,0:T(8,128)(2,1)S(1)}, u32[]{:S(2)}, u32[]{:S(2)}) collective-permute-start(bf16[2,2,128,128]{3,2,1,0:T(8,128)(2,1)S(1)} %pad_maximum_fusion), channel_id=1, source_target_pairs={{0,32},{8,40},{16,48},{24,56},{32,64},{40,72},{48,80},{56,88},{64,... | collective-permute-start | bytes 393224 | tf_op jit(solution)/shard_map/ppermute | solution.py:39
  10.5 6.2 %collective-permute-start.2 = (bf16[2,2,128,128]{3,2,1,0:T(8,128)(2,1)S(1)}, bf16[2,2,128,128]{3,2,1,0:T(8,128)(2,1)S(1)}, u32[]{:S(2)}, u32[]{:S(2)}) collective-permute-start(bf16[2,2,128,128]{3,2,1,0:T(8,128)(2,1)S(1)} %pad_maximum_fusion), channel_id=1, source_target_pairs={{0,96},{8,104},{16,112},{24,120},{32,0},{40,8},{48,16},{56,24},{64... | collective-permute-start | bytes 393224 | tf_op jit(solution)/shard_map/ppermute | solution.py:39
  14.8 6.5 %collective-permute-start.3 = (bf16[2,2,128,128]{3,2,1,0:T(8,128)(2,1)S(1)}, bf16[2,2,128,128]{3,2,1,0:T(8,128)(2,1)S(1)}, u32[]{:S(2)}, u32[]{:S(2)}) collective-permute-start(bf16[2,2,128,128]{3,2,1,0:T(8,128)(2,1)S(1)} %pad_maximum_fusion), channel_id=1, source_target_pairs={{0,64},{8,72},{16,80},{24,88},{32,96},{40,104},{48,112},{56,120},{... | collective-permute-start | bytes 393224 | tf_op jit(solution)/shard_map/ppermute | solution.py:39
  21.3 2.0 collective-permute-start.4
  24.3 36.4 %copy-start = (bf16[128,768]{1,0:T(8,128)(2,1)S(1)}, bf16[128,768]{1,0:T(8,128)(2,1)}, u32[]{:S(2)}) copy-start(bf16[128,768]{1,0:T(8,128)(2,1)} %residual_ref.1) | copy-start | bytes 589828
  34.3 26.4 %all-to-all-start = ((bf16[8,128,768]{2,1,0:T(8,128)(2,1)}), bf16[8,128,768]{2,1,0:T(8,128)(2,1)S(1)}, u32[]{:S(2)}, u32[]{:S(2)}) async-start(bf16[8,128,768]{2,1,0:T(8,128)(2,1)} %shard_map.109), calls=%async_computation | async-start | bytes 3145728 | tf_op jit(solution)/shard_map/all_to_all | solution.py:394
  83.3 21.7 %collective-permute-start.10 = (bf16[8,80,768]{2,1,0:T(8,128)(2,1)S(1)}, bf16[8,80,768]{2,1,0:T(8,128)(2,1)S(1)}, u32[]{:S(2)}, u32[]{:S(2)}) collective-permute-start(bf16[8,80,768]{2,1,0:T(8,128)(2,1)S(1)} %shard_map.112.refs_0_), channel_id=1, source_target_pairs={{0,96},{8,104},{16,112},{24,120},{32,0},{40,8},{48,16},{56,24},{64... | collective-permute-start | bytes 2949128 | tf_op jit(solution)/shard_map/ppermute | solution.py:39
  85.2 22.5 %collective-permute-start.9 = (bf16[8,80,768]{2,1,0:T(8,128)(2,1)S(1)}, bf16[8,80,768]{2,1,0:T(8,128)(2,1)S(1)}, u32[]{:S(2)}, u32[]{:S(2)}) collective-permute-start(bf16[8,80,768]{2,1,0:T(8,128)(2,1)S(1)} %shard_map.112.refs_0_), channel_id=1, source_target_pairs={{0,32},{8,40},{16,48},{24,56},{32,64},{40,72},{48,80},{56,88},{64,... | collective-permute-start | bytes 2949128 | tf_op jit(solution)/shard_map/ppermute | solution.py:39
  85.4 23.2 %collective-permute-start.8 = (bf16[8,80,768]{2,1,0:T(8,128)(2,1)S(1)}, bf16[8,80,768]{2,1,0:T(8,128)(2,1)S(1)}, u32[]{:S(2)}, u32[]{:S(2)}) collective-permute-start(bf16[8,80,768]{2,1,0:T(8,128)(2,1)S(1)} %shard_map.112.refs_0_), channel_id=1, source_target_pairs={{0,16},{8,24},{16,0},{24,8},{32,48},{40,56},{48,32},{56,40},{64,80... | collective-permute-start | bytes 2949128 | tf_op jit(solution)/shard_map/ppermute | solution.py:39
  108.8 27.4 %collective-permute-start.14 = (bf16[5,80,768]{2,1,0:T(8,128)(2,1)S(1)}, bf16[5,80,768]{2,1,0:T(8,128)(2,1)S(1)}, u32[]{:S(2)}, u32[]{:S(2)}) collective-permute-start(bf16[5,80,768]{2,1,0:T(8,128)(2,1)S(1)} %get-tuple-element.46), channel_id=1, source_target_pairs={{0,96},{8,104},{16,112},{24,120},{32,0},{40,8},{48,16},{56,24},{64... | collective-permute-start | bytes 1843208 | tf_op jit(solution)/shard_map/ppermute | solution.py:39
  111.8 24.4 %collective-permute-start.13 = (bf16[5,80,768]{2,1,0:T(8,128)(2,1)S(1)}, bf16[5,80,768]{2,1,0:T(8,128)(2,1)S(1)}, u32[]{:S(2)}, u32[]{:S(2)}) collective-permute-start(bf16[5,80,768]{2,1,0:T(8,128)(2,1)S(1)} %get-tuple-element.46), channel_id=1, source_target_pairs={{0,32},{8,40},{16,48},{24,56},{32,64},{40,72},{48,80},{56,88},{64,... | collective-permute-start | bytes 1843208 | tf_op jit(solution)/shard_map/ppermute | solution.py:39
  111.8 24.4 %collective-permute-start.11 = (bf16[4,80,768]{2,1,0:T(8,128)(2,1)S(1)}, bf16[4,80,768]{2,1,0:T(8,128)(2,1)S(1)}, u32[]{:S(2)}, u32[]{:S(2)}) collective-permute-start(bf16[4,80,768]{2,1,0:T(8,128)(2,1)S(1)} %get-tuple-element.44), channel_id=1, source_target_pairs={{0,32},{8,40},{16,48},{24,56},{32,64},{40,72},{48,80},{56,88},{64,... | collective-permute-start | bytes 1474568 | tf_op jit(solution)/shard_map/ppermute | solution.py:39
  111.8 24.4 %collective-permute-start.12 = (bf16[4,80,768]{2,1,0:T(8,128)(2,1)S(1)}, bf16[4,80,768]{2,1,0:T(8,128)(2,1)S(1)}, u32[]{:S(2)}, u32[]{:S(2)}) collective-permute-start(bf16[4,80,768]{2,1,0:T(8,128)(2,1)S(1)} %get-tuple-element.45), channel_id=1, source_target_pairs={{0,96},{8,104},{16,112},{24,120},{32,0},{40,8},{48,16},{56,24},{64... | collective-permute-start | bytes 1474568 | tf_op jit(solution)/shard_map/ppermute | solution.py:39
  115.1 21.1 %collective-permute-start.15 = (bf16[6,80,768]{2,1,0:T(8,128)(2,1)S(1)}, bf16[6,80,768]{2,1,0:T(8,128)(2,1)S(1)}, u32[]{:S(2)}, u32[]{:S(2)}) collective-permute-start(bf16[6,80,768]{2,1,0:T(8,128)(2,1)S(1)} %get-tuple-element.47), channel_id=1, source_target_pairs={{0,16},{8,24},{16,0},{24,8},{32,48},{40,56},{48,32},{56,40},{64,80... | collective-permute-start | bytes 2211848 | tf_op jit(solution)/shard_map/ppermute | solution.py:39
  136.3 19.8 %collective-permute-start.16 = (bf16[3,80,768]{2,1,0:T(8,128)(2,1)S(1)}, bf16[3,80,768]{2,1,0:T(8,128)(2,1)S(1)}, u32[]{:S(2)}, u32[]{:S(2)}) collective-permute-start(bf16[3,80,768]{2,1,0:T(8,128)(2,1)S(1)} %get-tuple-element.48), channel_id=1, source_target_pairs={{0,32},{8,40},{16,48},{24,56},{32,64},{40,72},{48,80},{56,88},{64,... | collective-permute-start | bytes 1105928 | tf_op jit(solution)/shard_map/ppermute | solution.py:39
  136.4 19.7 %collective-permute-start.18 = (bf16[3,80,768]{2,1,0:T(8,128)(2,1)S(1)}, bf16[3,80,768]{2,1,0:T(8,128)(2,1)S(1)}, u32[]{:S(2)}, u32[]{:S(2)}) collective-permute-start(bf16[3,80,768]{2,1,0:T(8,128)(2,1)S(1)} %get-tuple-element.50), channel_id=1, source_target_pairs={{0,16},{8,24},{16,0},{24,8},{32,48},{40,56},{48,32},{56,40},{64,80... | collective-permute-start | bytes 1105928 | tf_op jit(solution)/shard_map/ppermute | solution.py:39
  139.7 16.4 %collective-permute-start.17 = (bf16[2,80,768]{2,1,0:T(8,128)(2,1)S(1)}, bf16[2,80,768]{2,1,0:T(8,128)(2,1)S(1)}, u32[]{:S(2)}, u32[]{:S(2)}) collective-permute-start(bf16[2,80,768]{2,1,0:T(8,128)(2,1)S(1)} %get-tuple-element.49), channel_id=1, source_target_pairs={{0,96},{8,104},{16,112},{24,120},{32,0},{40,8},{48,16},{56,24},{64... | collective-permute-start | bytes 737288 | tf_op jit(solution)/shard_map/ppermute | solution.py:39
  169.4 12.7 %collective-permute-start.19 = (bf16[3,80,768]{2,1,0:T(8,128)(2,1)S(1)}, bf16[3,80,768]{2,1,0:T(8,128)(2,1)S(1)}, u32[]{:S(2)}, u32[]{:S(2)}) collective-permute-start(bf16[3,80,768]{2,1,0:T(8,128)(2,1)S(1)} %get-tuple-element.54), channel_id=1, source_target_pairs={{0,32},{8,40},{16,48},{24,56},{32,64},{40,72},{48,80},{56,88},{64,... | collective-permute-start | bytes 1105928 | tf_op jit(solution)/shard_map/ppermute | solution.py:39
  169.5 13.1 %collective-permute-start.21 = (bf16[3,80,768]{2,1,0:T(8,128)(2,1)S(1)}, bf16[3,80,768]{2,1,0:T(8,128)(2,1)S(1)}, u32[]{:S(2)}, u32[]{:S(2)}) collective-permute-start(bf16[3,80,768]{2,1,0:T(8,128)(2,1)S(1)} %get-tuple-element.56), channel_id=1, source_target_pairs={{0,16},{8,24},{16,0},{24,8},{32,48},{40,56},{48,32},{56,40},{64,80... | collective-permute-start | bytes 1105928 | tf_op jit(solution)/shard_map/ppermute | solution.py:39
  169.9 10.0 %collective-permute-start.20 = (bf16[2,80,768]{2,1,0:T(8,128)(2,1)S(1)}, bf16[2,80,768]{2,1,0:T(8,128)(2,1)S(1)}, u32[]{:S(2)}, u32[]{:S(2)}) collective-permute-start(bf16[2,80,768]{2,1,0:T(8,128)(2,1)S(1)} %get-tuple-element.55), channel_id=1, source_target_pairs={{0,96},{8,104},{16,112},{24,120},{32,0},{40,8},{48,16},{56,24},{64... | collective-permute-start | bytes 737288 | tf_op jit(solution)/shard_map/ppermute | solution.py:39
  173.6 17.0 %collective-permute-start.26 = (bf16[6,80,768]{2,1,0:T(8,128)(2,1)S(1)}, bf16[6,80,768]{2,1,0:T(8,128)(2,1)S(1)}, u32[]{:S(2)}, u32[]{:S(2)}) collective-permute-start(bf16[6,80,768]{2,1,0:T(8,128)(2,1)S(1)} %get-tuple-element.61), channel_id=1, source_target_pairs={{0,16},{8,24},{16,0},{24,8},{32,48},{40,56},{48,32},{56,40},{64,80... | collective-permute-start | bytes 2211848 | tf_op jit(solution)/shard_map/ppermute | solution.py:39
  182.9 24.1 %collective-permute-start.22 = (bf16[5,80,768]{2,1,0:T(8,128)(2,1)S(1)}, bf16[5,80,768]{2,1,0:T(8,128)(2,1)S(1)}, u32[]{:S(2)}, u32[]{:S(2)}) collective-permute-start(bf16[5,80,768]{2,1,0:T(8,128)(2,1)S(1)} %get-tuple-element.57), channel_id=1, source_target_pairs={{0,32},{8,40},{16,48},{24,56},{32,64},{40,72},{48,80},{56,88},{64,... | collective-permute-start | bytes 1843208 | tf_op jit(solution)/shard_map/ppermute | solution.py:39
  184.5 22.5 %collective-permute-start.23 = (bf16[5,80,768]{2,1,0:T(8,128)(2,1)S(1)}, bf16[5,80,768]{2,1,0:T(8,128)(2,1)S(1)}, u32[]{:S(2)}, u32[]{:S(2)}) collective-permute-start(bf16[5,80,768]{2,1,0:T(8,128)(2,1)S(1)} %get-tuple-element.58), channel_id=1, source_target_pairs={{0,96},{8,104},{16,112},{24,120},{32,0},{40,8},{48,16},{56,24},{64... | collective-permute-start | bytes 1843208 | tf_op jit(solution)/shard_map/ppermute | solution.py:39
  186.5 20.5 %collective-permute-start.24 = (bf16[4,80,768]{2,1,0:T(8,128)(2,1)S(1)}, bf16[4,80,768]{2,1,0:T(8,128)(2,1)S(1)}, u32[]{:S(2)}, u32[]{:S(2)}) collective-permute-start(bf16[4,80,768]{2,1,0:T(8,128)(2,1)S(1)} %get-tuple-element.59), channel_id=1, source_target_pairs={{0,32},{8,40},{16,48},{24,56},{32,64},{40,72},{48,80},{56,88},{64,... | collective-permute-start | bytes 1474568 | tf_op jit(solution)/shard_map/ppermute | solution.py:39
  187.5 19.6 %collective-permute-start.25 = (bf16[4,80,768]{2,1,0:T(8,128)(2,1)S(1)}, bf16[4,80,768]{2,1,0:T(8,128)(2,1)S(1)}, u32[]{:S(2)}, u32[]{:S(2)}) collective-permute-start(bf16[4,80,768]{2,1,0:T(8,128)(2,1)S(1)} %get-tuple-element.60), channel_id=1, source_target_pairs={{0,96},{8,104},{16,112},{24,120},{32,0},{40,8},{48,16},{56,24},{64... | collective-permute-start | bytes 1474568 | tf_op jit(solution)/shard_map/ppermute | solution.py:39
  207.7 15.8 %collective-permute-start.27 = (bf16[8,80,768]{2,1,0:T(8,128)(2,1)S(1)}, bf16[8,80,768]{2,1,0:T(8,128)(2,1)S(1)}, u32[]{:S(2)}, u32[]{:S(2)}) collective-permute-start(bf16[8,80,768]{2,1,0:T(8,128)(2,1)S(1)} %get-tuple-element.62), channel_id=1, source_target_pairs={{0,32},{8,40},{16,48},{24,56},{32,64},{40,72},{48,80},{56,88},{64,... | collective-permute-start | bytes 2949128 | tf_op jit(solution)/shard_map/ppermute | solution.py:39
  208.6 14.9 %collective-permute-start.28 = (bf16[8,80,768]{2,1,0:T(8,128)(2,1)S(1)}, bf16[8,80,768]{2,1,0:T(8,128)(2,1)S(1)}, u32[]{:S(2)}, u32[]{:S(2)}) collective-permute-start(bf16[8,80,768]{2,1,0:T(8,128)(2,1)S(1)} %get-tuple-element.63), channel_id=1, source_target_pairs={{0,96},{8,104},{16,112},{24,120},{32,0},{40,8},{48,16},{56,24},{64... | collective-permute-start | bytes 2949128 | tf_op jit(solution)/shard_map/ppermute | solution.py:39
  211.1 20.9 %collective-permute-start.29 = (bf16[8,80,768]{2,1,0:T(8,128)(2,1)S(1)}, bf16[8,80,768]{2,1,0:T(8,128)(2,1)S(1)}, u32[]{:S(2)}, u32[]{:S(2)}) collective-permute-start(bf16[8,80,768]{2,1,0:T(8,128)(2,1)S(1)} %get-tuple-element.64), channel_id=1, source_target_pairs={{0,16},{8,24},{16,0},{24,8},{32,48},{40,56},{48,32},{56,40},{64,80... | collective-permute-start | bytes 2949128 | tf_op jit(solution)/shard_map/ppermute | solution.py:39
  (4 other events, 45.5 us)
